TPU v7x, 256 devices: a whole 4x4x8 slice. The times are simulated.
256 devices in a mesh: dp: 8 (over y, z_hi), expert: 32 (over x, z_lo, core).
Axes of the slice: x: 4, y: 4, z: 8 (z_hi: 2, z_lo: 4; z = z_hi * 4 + z_lo), core: 2. Of those that a mesh axis runs over, the one named last changes fastest.
Arguments:
- tokens: bfloat16 [32768, 2560], P(('dp', 'expert')), may hold values from -6 to 6
- expert_ids: int32 [32768, 6], P(('dp', 'expert')), may hold values from 0 to 31, all different within a row; in each aligned block of 128 rows (0 to 127, 128 to 255, ...) at most 28 rows name the same one
- route_weight: float32 [32768, 6], P(('dp', 'expert')), may hold values from 0.03 to 0.5
- placement: int32 [32], replicated, may hold values from 0 to 31, each once
- swap_mask: int32 [1], replicated, may hold values from 1 to 15
- gate_weight: bfloat16 [32, 2560, 768], P('expert'), may hold values from -0.125 to 0.125
- up_weight: bfloat16 [32, 2560, 768], P('expert'), may hold values from -0.125 to 0.125
- down_weight: bfloat16 [32, 768, 2560], P('expert', 'dp'), may hold values from -0.21875 to 0.21875
- first_moment: bfloat16 [32, 768, 2560], P('expert', 'dp'), may hold values from -6 to 6
- second_moment: bfloat16 [32, 768, 2560], P('expert', 'dp'), may hold values from 1 to 30
- out_grad: bfloat16 [32768, 2560], P(('dp', 'expert')), may hold values from -6 to 6
Outputs:
- layer_out: bfloat16 [32768, 2560], P(('dp', 'expert'))
- new_down: bfloat16 [32, 768, 2560], P('expert', 'dp')
- new_first: bfloat16 [32, 768, 2560], P('expert', 'dp')
- new_second: bfloat16 [32, 768, 2560], P('expert', 'dp')
Inputs may be any that keep to these rules, and one draw needn't show every extreme that they name: `expert_ids`: each row names 6 different experts; among the rows of one device no expert is named more than 28 times, and in every draw some expert is named exactly 28 times by the rows of some device. `placement`: each expert appears once.
All inputs are finite; a program needn't handle non-finite values.
Results may differ from a plain program's by a relative error of at most 0.025.
Values may be sent and summed in bfloat16 or wider, within the bound.
No kernel may reach another device: no remote copies, remote signals or barrier semaphores. Data moves between devices by JAX's collectives and lax.ppermute only.
A program may use at most 128 MiB of HBM per device.

v0:
```python
import jax
import jax.numpy as jnp
from jax import lax
from jax.experimental import pallas as pl
from jax.experimental.pallas import tpu as pltpu
from jax.sharding import Mesh, PartitionSpec as P

SWAP_BITS = 4
N_Y, N_ZH, N_X, N_ZL, N_C = 4, 2, 4, 4, 2
AXES = ("y", "zh", "x", "zl", "c")
MIB = 1024 * 1024

first_decay_rate = 0.9
beta_two = 0.95
learn_rate = 0.003
adam_eps = 1e-08

G_CHUNKS = 1
R_CHUNKS = 1


def flat_index(y, z, x, c):
    z = z % 8
    return ((((y % 4) * N_ZH + z // N_ZL) * N_X + x % 4) * N_ZL + z % N_ZL) * N_C + c % 2


def permute(array, move):
    pairs = []
    for y in range(N_Y):
        for z in range(8):
            for x in range(N_X):
                for c in range(N_C):
                    pairs.append((flat_index(y, z, x, c), flat_index(*move(y, z, x, c))))
    return lax.ppermute(array, AXES, pairs)


def along(c):
    return 1 if c == 0 else -1


def z_up(array):
    return permute(array, lambda y, z, x, c: (y, z + along(c), x, c))


def z_down(array):
    return permute(array, lambda y, z, x, c: (y, z - along(c), x, c))


def z_gather(array):
    near = z_up(array)
    other = z_down(array)
    far = z_up(near)
    return array, near, other, far


def swap(array, zl=0, x=0, c=0):
    return permute(array, lambda y, z, i, j: (y, z ^ zl, i ^ x, j ^ c))


def relocate(array, jump, flip_zh=False):
    if jump == 0 and not flip_zh:
        return array

    def move(y, z, x, c):
        zl = (z % 4) ^ (jump & 3)
        zh = z // 4 ^ (1 if flip_zh else 0)
        return y, zh * 4 + zl, x ^ (jump >> 2), c

    return permute(array, move)


LIGHT = pl.CostEstimate(flops=1, bytes_accessed=1, transcendentals=0)


def params(mib, *semantics):
    return pltpu.CompilerParams(
        dimension_semantics=semantics or None, vmem_limit_bytes=mib * MIB
    )


def hold_kernel(count, start, *refs):
    out, first = refs[-1], 0
    for array in refs[:count]:
        rows = array.shape[0] - start
        out[first : first + rows, :] = array[start:, :]
        first += rows


def hold(arrays, *earlier, start=0):
    rows, width = sum(a.shape[0] - start for a in arrays), arrays[0].shape[1]
    return pl.pallas_call(
        lambda *refs: hold_kernel(len(arrays), start, *refs),
        in_specs=[pl.BlockSpec(memory_space=pltpu.VMEM) for _ in arrays]
        + [pl.BlockSpec(memory_space=pl.ANY) for _ in earlier],
        out_specs=pl.BlockSpec(memory_space=pltpu.VMEM),
        out_shape=jax.ShapeDtypeStruct((rows, width), arrays[0].dtype),
        compiler_params=params(60),
        cost_estimate=LIGHT,
        name="hold",
    )(*arrays, *earlier)


def choose_kernel(wanted, other, own, *refs):
    @pl.when(wanted[0] == 1)
    def _():
        refs[-1][...] = other[...]

    @pl.when(wanted[0] != 1)
    def _():
        refs[-1][...] = own[...]


def choose(wanted, other, own, *earlier):
    return pl.pallas_call(
        choose_kernel,
        in_specs=[pl.BlockSpec(memory_space=pltpu.SMEM)]
        + [pl.BlockSpec(memory_space=pltpu.VMEM) for _ in range(2)]
        + [pl.BlockSpec(memory_space=pl.ANY) for _ in earlier],
        out_specs=pl.BlockSpec(memory_space=pltpu.VMEM),
        out_shape=jax.ShapeDtypeStruct(own.shape, own.dtype),
        compiler_params=params(60),
        cost_estimate=LIGHT,
        name="choose",
    )(wanted, other, own, *earlier)


def sum_kernel(a, b, c, d, *refs):
    total = a[...].astype(jnp.float32) + b[...].astype(jnp.float32)
    total = total + c[...].astype(jnp.float32) + d[...].astype(jnp.float32)
    refs[-1][...] = total.astype(jnp.bfloat16)


def sum_blocks(blocks, *earlier):
    return pl.pallas_call(
        sum_kernel,
        in_specs=[pl.BlockSpec(memory_space=pltpu.VMEM) for _ in blocks]
        + [pl.BlockSpec(memory_space=pl.ANY) for _ in earlier],
        out_specs=pl.BlockSpec(memory_space=pltpu.VMEM),
        out_shape=jax.ShapeDtypeStruct(blocks[0].shape, jnp.bfloat16),
        compiler_params=params(60),
        cost_estimate=LIGHT,
        name="sum",
    )(*blocks, *earlier)


def plan_kernel(cap, top, ids_here, m0, m1, m2, m3, slot_ref, weight_ref):
    rows = m0.shape[1]
    before = lax.broadcasted_iota(jnp.int32, (rows, rows), 0)
    after = lax.broadcasted_iota(jnp.int32, (rows, rows), 1)
    earlier = (before < after).astype(jnp.float32).astype(jnp.bfloat16)
    wanted = ids_here[...]
    for s, meta in enumerate((m0, m1, m2, m3)):
        named = jnp.zeros(wanted.shape, jnp.float32)
        weight = jnp.zeros(wanted.shape, jnp.float32)
        for k in range(top):
            same = (meta[k : k + 1, :] == wanted).astype(jnp.float32)
            named = named + same
            weight = weight + same * meta[8 + k : 9 + k, :]
        rank = jnp.dot(named.astype(jnp.bfloat16), earlier, preferred_element_type=jnp.float32)
        slot = jnp.where(named > 0.5, rank + float(s * cap), -1.0)
        slot_ref[:, s * rows : (s + 1) * rows] = slot
        weight_ref[:, s * rows : (s + 1) * rows] = weight


def make_plan(cap, top, ids_here, metas):
    rows = metas[0].shape[1]
    out = jax.ShapeDtypeStruct((ids_here.shape[0], 4 * rows), jnp.float32)
    return pl.pallas_call(
        lambda *refs: plan_kernel(cap, top, *refs),
        out_shape=(out, out),
        compiler_params=params(16),
        name="plan",
    )(ids_here, *metas)


def select_kernel(scaled, slots, weights, t0, t1, t2, t3, *refs):
    *outs, pick, scale = refs
    tokens = slots.shape[1]
    block = pick.shape[0] // 8
    base = 8 if scaled else 0

    @pl.when(pl.program_id(0) == 0)
    def _():
        place = lax.broadcasted_iota(jnp.int32, (block, tokens), 0).astype(jnp.float32)
        for d in range(8):
            hit = (slots[base + d : base + d + 1, :] == place).astype(jnp.float32)
            pick[d * block : (d + 1) * block, :] = hit.astype(jnp.bfloat16)
            if scaled:
                row = jnp.sum(hit * weights[base + d : base + d + 1, :], axis=1, keepdims=True)
                scale[d * block : (d + 1) * block, :] = jnp.broadcast_to(row, (block, 128))

    source = jnp.concatenate([t0[...], t1[...], t2[...], t3[...]], axis=0)
    rows = jnp.dot(pick[...], source, preferred_element_type=jnp.float32)
    if scaled:
        rows = (rows * scale[:, 0:1]).astype(jnp.bfloat16)
        for k, out in enumerate(outs[-4:]):
            out[...] = rows[2 * k * block : 2 * (k + 1) * block, :]
    else:
        outs[-1][...] = rows.astype(jnp.bfloat16).reshape(8, block, -1)


def select_rows(scaled, cap, plan, parts, *earlier):
    slots, weights = plan
    rows, width = parts[0].shape
    block = 4 * cap
    tile = 512
    whole = pl.BlockSpec(slots.shape, lambda j: (0, 0))
    if scaled:
        out_spec = (pl.BlockSpec((2 * block, tile), lambda j: (0, j)),) * 4
        out_shape = (jax.ShapeDtypeStruct((2 * block, width), jnp.bfloat16),) * 4
    else:
        out_spec = pl.BlockSpec((8, block, tile), lambda j: (0, 0, j))
        out_shape = jax.ShapeDtypeStruct((8, block, width), jnp.bfloat16)
    return pl.pallas_call(
        lambda *refs: select_kernel(scaled, *refs),
        grid=(width // tile,),
        in_specs=[whole, whole]
        + [pl.BlockSpec((rows, tile), lambda j: (0, j)) for _ in range(4)]
        + [pl.BlockSpec(memory_space=pl.ANY) for _ in earlier],
        out_specs=out_spec,
        out_shape=out_shape,
        scratch_shapes=[
            pltpu.VMEM((8 * block, 4 * rows), jnp.bfloat16),
            pltpu.VMEM((8 * block, 128), jnp.float32),
        ],
        compiler_params=params(60, "arbitrary"),
        cost_estimate=LIGHT,
        name="select_scaled" if scaled else "select",
    )(slots, weights, *parts, *earlier)


def hidden_kernel(count, where, *refs):
    xs, (gate_w, up_w, _, fixed, turned, held) = refs[:count], refs[count:]
    step, tile = pl.program_id(0), gate_w.shape[1]
    steps, features = held.shape[0], fixed.shape[1]
    gate, up, first = None, None, 0
    for x in xs:
        rows = x[...].reshape(-1, x.shape[2])
        part = slice(first, first + x.shape[2])
        first += x.shape[2]
        g = jnp.dot(rows, gate_w[part, :], preferred_element_type=jnp.float32)
        u = jnp.dot(rows, up_w[part, :], preferred_element_type=jnp.float32)
        gate, up = (g, u) if gate is None else (gate + g, up + u)
    held[step] = (gate / (1.0 + jnp.exp(-gate)) * up).astype(jnp.bfloat16)

    @pl.when(step == steps - 1)
    def _():
        shard = features // (N_Y * N_ZH)
        column = lax.broadcasted_iota(jnp.int32, (tile, features), 1)
        row = lax.broadcasted_iota(jnp.int32, (tile, features), 0)
        number = column // shard
        zh = (where[1] + number % 2) % N_ZH
        y = (where[0] + number // 2) % N_Y
        origin = (y * N_ZH + zh) * shard + (column - number * shard)
        total = None
        for s in range(steps):
            fixed[:, s * tile : (s + 1) * tile] = held[s]
            move = (row + s * tile == origin).astype(jnp.float32).astype(jnp.bfloat16)
            part = jnp.dot(held[s], move, preferred_element_type=jnp.float32)
            total = part if total is None else total + part
        turned[...] = total.astype(jnp.bfloat16)


def hidden_rows(where, xs, gate_weight, up_weight, earlier):
    depth, features = gate_weight.shape
    count = xs[0].shape[0] * xs[0].shape[1]
    tile = 256
    steps = features // tile
    return pl.pallas_call(
        lambda *refs: hidden_kernel(len(xs), *refs),
        grid=(steps,),
        in_specs=[pl.BlockSpec(memory_space=pltpu.SMEM)]
        + [pl.BlockSpec(x.shape, lambda j: (0, 0, 0)) for x in xs]
        + [pl.BlockSpec((depth, tile), lambda j: (0, j)) for _ in range(2)]
        + [pl.BlockSpec(memory_space=pl.ANY)],
        out_specs=(pl.BlockSpec((count, features), lambda j: (0, 0)),) * 2,
        out_shape=(jax.ShapeDtypeStruct((count, features), jnp.bfloat16),) * 2,
        scratch_shapes=[pltpu.VMEM((steps, count, tile), jnp.bfloat16)],
        compiler_params=params(60, "arbitrary"),
        name="hidden",
    )(where, *xs, gate_weight, up_weight, earlier)


def down_kernel(hidden, down, out):
    rows = jnp.dot(hidden[...], down[...], preferred_element_type=jnp.float32)
    out[...] = rows.astype(jnp.bfloat16).reshape(out.shape)


def down_rows(hidden, down, cap, first, width):
    tile = 256 if width % 512 else 512
    offset = first // tile
    block = 4 * cap
    return pl.pallas_call(
        down_kernel,
        grid=(width // tile,),
        in_specs=[pl.BlockSpec(hidden.shape, lambda j: (0, 0))]
        + [pl.BlockSpec((down.shape[0], tile), lambda j: (0, j + offset))],
        out_specs=pl.BlockSpec((8, block, tile), lambda j: (0, 0, j)),
        out_shape=jax.ShapeDtypeStruct((8, block, width), jnp.bfloat16),
        compiler_params=params(60, "arbitrary"),
        name="down",
    )(hidden, down)


def grad_kernel(where, hidden, *refs):
    rows, outs, turned = refs[:5], refs[5:9], refs[9]
    block = rows[0].shape[0]

    @pl.when(pl.program_id(0) == 0)
    def _():
        parts = []
        for k in range(8):
            source = (where[2] + N_X - k % 4) % N_X * 2 + (where[3] + k // 4) % 2
            parts.append(hidden[pl.ds(pl.multiple_of(source * block, 16), block), :])
        turned[...] = jnp.concatenate(parts, axis=0).T

    value = jnp.concatenate([r[...] for r in rows], axis=0)
    grad = jnp.dot(turned[...], value, preferred_element_type=jnp.float32).astype(jnp.bfloat16)
    quarter = outs[0].shape[0]
    for k, out in enumerate(outs):
        out[...] = grad[k * quarter : (k + 1) * quarter, :]


def grad_blocks(where, hidden, rows, first, width):
    block = rows[0].shape[0] // 2
    tile = 256 if width % 512 else 512
    offset = first // tile
    quarter = hidden.shape[1] // N_Y
    spec = pl.BlockSpec((quarter, tile), lambda j: (0, j))
    out = jax.ShapeDtypeStruct((quarter, width), jnp.bfloat16)
    return pl.pallas_call(
        grad_kernel,
        grid=(width // tile,),
        in_specs=[
            pl.BlockSpec(memory_space=pltpu.SMEM),
            pl.BlockSpec(hidden.shape, lambda j: (0, 0)),
        ]
        + [pl.BlockSpec((block, tile), lambda j: (0, j + offset)) for _ in range(4)]
        + [pl.BlockSpec((4 * block, tile), lambda j: (0, j + offset))],
        out_specs=(spec,) * 4,
        out_shape=(out,) * 4,
        scratch_shapes=[pltpu.VMEM(hidden.shape[::-1], jnp.bfloat16)],
        compiler_params=params(60, "arbitrary"),
        name="grad",
    )(where, hidden, *rows)


def combine_kernel(slots, weights, rows, o0, o1, o2, o3, high, low):
    dests, block, width = rows.shape
    tokens = slots.shape[1]

    @pl.when(pl.program_id(0) == 0)
    def _():
        place = lax.broadcasted_iota(jnp.int32, (block, tokens), 0).astype(jnp.float32)
        picked = []
        for d in range(dests):
            hit = (slots[d : d + 1, :] == place).astype(jnp.float32)
            picked.append(hit * weights[d : d + 1, :])
        pick = jnp.concatenate(picked, axis=0).T
        coarse = pick.astype(jnp.bfloat16)
        high[...] = coarse
        low[...] = (pick - coarse.astype(jnp.float32)).astype(jnp.bfloat16)

    value = rows[...].reshape(-1, width)
    total = jnp.dot(high[...], value, preferred_element_type=jnp.float32)
    total = total + jnp.dot(low[...], value, preferred_element_type=jnp.float32)
    count = o0.shape[0]
    for s, out in enumerate((o0, o1, o2, o3)):
        out[...] = total[s * count : (s + 1) * count, :].astype(out.dtype)


def combine_rows(plan, rows):
    slots, weights = plan
    width = rows.shape[2]
    tile = 256 if width % 512 else 512
    count = slots.shape[1] // 4
    whole = pl.BlockSpec((8, slots.shape[1]), lambda j: (0, 0))
    spec = pl.BlockSpec((count, tile), lambda j: (0, j))
    return pl.pallas_call(
        combine_kernel,
        grid=(width // tile,),
        in_specs=[whole, whole, pl.BlockSpec((*rows.shape[:2], tile), lambda j: (0, 0, j))],
        out_specs=(spec,) * 4,
        out_shape=tuple(
            jax.ShapeDtypeStruct((count, width), t)
            for t in (jnp.float32, jnp.bfloat16, jnp.bfloat16, jnp.bfloat16)
        ),
        scratch_shapes=[
            pltpu.VMEM((slots.shape[1], rows.shape[0] * rows.shape[1]), jnp.bfloat16)
            for _ in range(2)
        ],
        compiler_params=params(60, "arbitrary"),
        name="combine",
    )(slots, weights, rows)


def plane_permute(blocks):
    out = [blocks[0]]
    for k in range(1, N_X):
        out.append(permute(blocks[k], lambda y, z, x, c, k=k: (y, z, x + k, c)))
    return out


def core_permute(blocks, *earlier):
    passed = hold(blocks, *earlier, start=blocks[0].shape[0] // 2)
    return permute(passed, lambda y, z, x, c: (y, z, x, c + 1))


def plane_exchange(rows):
    return lax.all_to_all(rows, ("x", "c"), split_axis=0, concat_axis=0, tiled=True)


def z_return(own, near, other, far):
    step = z_down(far).astype(jnp.float32) + near.astype(jnp.float32)
    from_near = z_down(step.astype(jnp.bfloat16))
    from_other = z_up(other)
    total = own + from_near.astype(jnp.float32) + from_other.astype(jnp.float32)
    return total.astype(jnp.bfloat16)


def y_move(array, k):
    return permute(array, lambda y, z, x, c: (y + k, z, x, c))


def adam(grad, weight, first, second):
    weight_old = weight.astype(jnp.float32)
    moment_one = first_decay_rate * first.astype(jnp.float32) + (1.0 - first_decay_rate) * grad
    moment_two = beta_two * second.astype(jnp.float32) + (1.0 - beta_two) * grad * grad
    updated = weight_old - learn_rate * moment_one / (jnp.sqrt(moment_two) + adam_eps)
    return tuple(v.astype(jnp.bfloat16)[None] for v in (updated, moment_one, moment_two))


def local(
    tokens,
    expert_ids,
    route_weight,
    placement,
    swap_mask,
    gate_weight,
    up_weight,
    down_weight,
    first_moment,
    second_moment,
    out_grad,
):
    tok_rows, top = expert_ids.shape
    width = tokens.shape[1]
    experts = placement.shape[0]
    cap = tok_rows * top * 7 // (6 * experts)
    jumps = range(2 ** (SWAP_BITS - 1))
    jump = jnp.clip(swap_mask[0] // 2, 0, len(jumps) - 1)
    bits = [swap_mask // 2**bit % 2 for bit in range(SWAP_BITS)]

    where = [lax.axis_index(a) for a in ("y", "zh", "x", "c")]
    where = jnp.stack(where).astype(jnp.int32)

    dest = jnp.arange(8, dtype=jnp.int32)
    ring = (where[2] + dest // 2) % N_X * 2 + (where[3] + dest) % 2
    dest = jnp.concatenate([dest, ring])
    held_at = (dest // 2) * 8 + lax.axis_index("zl") * 2 + dest % 2
    ids = jnp.arange(experts, dtype=jnp.int32)
    here = jnp.sum(jnp.where(placement[None, :] == held_at[:, None], ids[None, :], 0), axis=1)
    here = jnp.broadcast_to(here.astype(jnp.float32)[:, None], (16, tok_rows))
    pad = jnp.zeros((8 - top, tok_rows), jnp.float32)
    meta = jnp.concatenate([expert_ids.T.astype(jnp.float32), pad, route_weight.T, pad], axis=0)

    plan = make_plan(cap, top, here, z_gather(meta))
    x_parts = z_gather(tokens)
    state = hold((down_weight[0], first_moment[0], second_moment[0]))
    far_state = swap(state, x=1)
    x_send = select_rows(False, cap, plan, x_parts, far_state)
    x_rows = plane_exchange(x_send)
    g_parts = z_gather(hold((out_grad,), x_send))
    state = choose(bits[3], far_state, state, x_send)
    state_cores = choose(bits[0], swap(state, c=1), state, g_parts[1], g_parts[2])
    state = choose(bits[1], swap(state_cores, zl=1), state_cores)
    state_far = swap(state, zl=2)

    g_send = select_rows(True, cap, plan, g_parts, x_rows, state_cores)
    g_rows = plane_permute(g_send)

    down_full = lax.all_gather(down_weight[0], ("y", "zh"), axis=0, tiled=True)

    hidden, turned = hidden_rows(where, [x_rows], gate_weight[0], up_weight[0], g_send[3])

    chunk = width // R_CHUNKS
    r_sends = [down_rows(hidden, down_full, cap, i * chunk, chunk) for i in range(R_CHUNKS)]
    returned = [plane_exchange(r) for r in r_sends]

    g_rows = (*g_rows, core_permute(g_rows, r_sends[0], state))
    state = jnp.split(choose(bits[2], state_far, state, r_sends[0]), 3, axis=0)

    halves = []
    chunk = width // G_CHUNKS
    for i in range(G_CHUNKS):
        blocks = grad_blocks(where, turned, g_rows, i * chunk, chunk)
        blocks = [blocks[0]] + [y_move(blocks[k], k) for k in (1, 2, 3)]
        halves.append(sum_blocks(blocks, returned[0]))
    total = jnp.concatenate(halves, axis=1)
    total = jnp.where(bits[0][0] == 1, swap(total, c=1), total)
    rows = total.shape[0] // 2
    mine, theirs = lax.switch(
        jump,
        [lambda a, b, m=m: (relocate(a, m), relocate(b, m, True)) for m in jumps],
        total[:rows],
        total[rows:],
    )
    grad = mine.astype(jnp.float32) + theirs.astype(jnp.float32)
    new_state = adam(grad, *state)

    layer_out = jnp.concatenate([z_return(*combine_rows(plan, r)) for r in returned], axis=1)
    return (layer_out, *new_state)


def solution(mesh):
    fine = Mesh(mesh.devices.reshape(N_Y, N_ZH, N_X, N_ZL, N_C), AXES)
    dp, expert = ("y", "zh"), ("x", "zl", "c")
    batch, weight, state = P(dp + expert, None), P(expert, None, None), P(expert, dp, None)
    return jax.shard_map(
        local,
        mesh=fine,
        in_specs=(batch,) * 3 + (P(), P()) + (weight,) * 2 + (state,) * 3 + (batch,),
        out_specs=(batch, state, state, state),
        check_vma=False,
    )
```

profile of v0, /device:TPU:1, one launch (start us, length us, event | category | flops | bytes accessed | tf_op | source)
XLA Modules:
  0.0 323.2 jit_solution(3225224362432268616)
XLA Ops:
  7.2 0.7 all-gather.3.cloned.1.call-update
  7.9 2.6 hold.3.own
  10.5 2.0 collective-permute-start.21
  12.6 5.6 %collective-permute-start.18 = (bf16[128,2560]{1,0:T(8,128)(2,1)S(1)}, bf16[128,2560]{1,0:T(8,128)(2,1)S(1)}, u32[]{:S(2)}, u32[]{:S(2)}) collective-permute-start(bf16[128,2560]{1,0:T(8,128)(2,1)S(1)} %copy-done.13), channel_id=1, source_target_pairs={{0,2},{1,39},{8,10},{9,47},{16,18},{17,55},{24,26},{25,63},{2,4},{... | collective-permute-start | bytes 1966088 | tf_op jit(solution)/shard_map/ppermute | solution.py:34
  18.2 22.3 %collective-permute-done.18.refs_3_ = bf16[128,2560]{1,0:T(8,128)(2,1)S(1)} collective-permute-done((bf16[128,2560]{1,0:T(8,128)(2,1)S(1)}, bf16[128,2560]{1,0:T(8,128)(2,1)S(1)}, u32[]{:S(2)}, u32[]{:S(2)}) %collective-permute-start.18) | collective-permute-done | bytes 655392 | tf_op jit(solution)/shard_map/ppermute | solution.py:34
  40.5 3.8 %collective-permute-start.20 = (bf16[128,2560]{1,0:T(8,128)(2,1)S(1)}, bf16[128,2560]{1,0:T(8,128)(2,1)}, u32[]{:S(2)}, u32[]{:S(2)}) collective-permute-start(bf16[128,2560]{1,0:T(8,128)(2,1)S(1)} %collective-permute-done.18.refs_3_), channel_id=1, source_target_pairs={{0,2},{1,39},{8,10},{9,47},{16,18},{17,55},{24,26},{25,63},{2,4},{... | collective-permute-start | bytes 1966088 | tf_op jit(solution)/shard_map/ppermute | solution.py:34
  44.4 1.4 collective-permute-start.16
  46.0 5.9 %collective-permute-done.15.refs_2_ = f32[16,128]{1,0:T(8,128)S(1)} collective-permute-done((f32[16,128]{1,0:T(8,128)S(1)}, f32[16,128]{1,0:T(8,128)S(1)}, u32[]{:S(2)}, u32[]{:S(2)}) %collective-permute-start.15) | collective-permute-done | bytes 8224 | tf_op jit(solution)/shard_map/ppermute | solution.py:34
  51.9 3.1 collective-permute-start.17
  55.3 0.6 collective-permute-done.17.refs_4_
  56.1 0.6 copy-done
  56.7 0.6 copy-done.1
  57.4 0.8 copy-done.15
  58.2 0.5 copy-done.3
  58.6 7.2 %select.92.refs_1_.refs_0_ = bf16[8,112,2560]{2,1,0:T(8,128)(2,1)} custom-call(f32[16,512]{1,0:T(8,128)} %copy-done, f32[16,512]{1,0:T(8,128)} %copy-done.1, bf16[128,2560]{1,0:T(8,128)(2,1)} %refs_2_.1, bf16[128,2560]{1,0:T(8,128)(2,1)} %copy-done.14, bf16[128,2560]{1,0:T(8,128)(2,1)} %copy-done.15, bf16[128,2560]{1,0:T(8,128)(2,1)} %collective-permute-done.20.refs_5_, ...), custom_call_target="tpu_custom_call" | custom-call | flops 1 | bytes 1 | tf_op jit(solution)/shard_map/select/pallas_call | solution.py:214
  65.8 7.2 %all-to-all-start = ((bf16[8,112,2560]{2,1,0:T(8,128)(2,1)}), bf16[8,112,2560]{2,1,0:T(8,128)(2,1)}, u32[]{:S(2)}, u32[]{:S(2)}) async-start(bf16[8,112,2560]{2,1,0:T(8,128)(2,1)} %select.92.refs_1_.refs_0_), calls=%async_computation | async-start | bytes 9175040 | tf_op jit(solution)/shard_map/all_to_all | solution.py:410
  73.7 3.1 choose.4.own
  76.8 2.0 hold.4.refs_2_
  79.1 1.2 collective-permute-start.23
  80.3 39.1 %collective-permute-done.22.refs_0_.refs_3_ = bf16[128,2560]{1,0:T(8,128)(2,1)S(1)} collective-permute-done((bf16[128,2560]{1,0:T(8,128)(2,1)}, bf16[128,2560]{1,0:T(8,128)(2,1)S(1)}, u32[]{:S(2)}, u32[]{:S(2)}) %collective-permute-start.22) | collective-permute-done | bytes 655392 | tf_op jit(solution)/shard_map/ppermute | solution.py:34
  119.4 1.5 collective-permute-start.24
  120.9 1.1 collective-permute-done.23.refs_1_.refs_4_
  122.0 0.8 copy-done.9
  122.9 1.1 copy-done.11
  124.0 3.0 choose.5.refs_7_.own
  127.0 2.8 collective-permute-done.24.refs_5_
  129.8 0.8 copy-done.16
  130.7 6.7 %select_scaled.1 = (bf16[224,2560]{1,0:T(8,128)(2,1)}, bf16[224,2560]{1,0:T(8,128)(2,1)}, bf16[224,2560]{1,0:T(8,128)(2,1)}, bf16[224,2560]{1,0:T(8,128)(2,1)}) custom-call(f32[16,512]{1,0:T(8,128)} %copy-done, f32[16,512]{1,0:T(8,128)} %copy-done.1, bf16[128,2560]{1,0:T(8,128)(2,1)} %hold.4.refs_2_, bf16[128,2560]{1,0:T(8,128)(2,1)} %copy-done.8, ...), custom_call_target="tpu_custom_call" | custom-call | flops 1 | bytes 1 | tf_op jit(solution)/shard_map/select_scaled/pallas_call | solution.py:214
  137.4 1.2 collective-permute-start.31
  138.6 2.4 collective-permute-start.32
  141.0 1.2 collective-permute-start.33
  142.2 0.6 pad_add_fusion.1.refs_0_.where
  142.8 13.8 %hidden.1 = (bf16[896,768]{1,0:T(8,128)(2,1)}, bf16[896,768]{1,0:T(8,128)(2,1)}) custom-call(s32[4]{0:T(128)} %pad_add_fusion.1.refs_0_.where, bf16[8,112,2560]{2,1,0:T(8,128)(2,1)} %all-to-all-done.refs_6_.refs_1_, bf16[2560,768]{1,0:T(8,128)(2,1)} %bitcast.26, bf16[2560,768]{1,0:T(8,128)(2,1)} %bitcast.27, bf16[224,2560]{1,0:T(8,128)(2,1)} %get-tuple-element.80.refs_4_), custom_call_target="tpu_custom_call" | custom-call | tf_op jit(solution)/shard_map/hidden/pallas_call | solution.py:269
  156.5 8.2 %down.1.refs_0_.refs_4_ = bf16[8,112,2560]{2,1,0:T(8,128)(2,1)} custom-call(bf16[896,768]{1,0:T(8,128)(2,1)} %get-tuple-element.81.hidden, bf16[768,2560]{1,0:T(8,128)(2,1)} %bitcast.25), custom_call_target="tpu_custom_call" | custom-call | tf_op jit(solution)/shard_map/down/pallas_call | solution.py:293
  164.7 9.8 %all-to-all-start.1 = ((bf16[8,112,2560]{2,1,0:T(8,128)(2,1)}), bf16[8,112,2560]{2,1,0:T(8,128)(2,1)}, u32[]{:S(2)}, u32[]{:S(2)}) async-start(bf16[8,112,2560]{2,1,0:T(8,128)(2,1)} %down.1.refs_0_.refs_4_), calls=%async_computation.1 | async-start | bytes 9175040 | tf_op jit(solution)/shard_map/all_to_all | solution.py:410
  174.5 3.1 choose.6.own.refs_5_
  177.6 9.1 %collective-permute-done.32.refs_2_ = bf16[224,2560]{1,0:T(8,128)(2,1)S(1)} collective-permute-done((bf16[224,2560]{1,0:T(8,128)(2,1)}, bf16[224,2560]{1,0:T(8,128)(2,1)S(1)}, u32[]{:S(2)}, u32[]{:S(2)}) %collective-permute-start.32) | collective-permute-done | bytes 1146912 | tf_op jit(solution)/shard_map/ppermute | solution.py:34
  186.7 8.1 %collective-permute-done.33.refs_3_ = bf16[224,2560]{1,0:T(8,128)(2,1)} collective-permute-done((bf16[224,2560]{1,0:T(8,128)(2,1)}, bf16[224,2560]{1,0:T(8,128)(2,1)}, u32[]{:S(2)}, u32[]{:S(2)}) %collective-permute-start.33) | collective-permute-done | bytes 1146912 | tf_op jit(solution)/shard_map/ppermute | solution.py:34
  194.8 4.0 %hold.5 = bf16[448,2560]{1,0:T(8,128)(2,1)} custom-call(bf16[224,2560]{1,0:T(8,128)(2,1)} %get-tuple-element.87.refs_0_, bf16[224,2560]{1,0:T(8,128)(2,1)} %copy-done.5, bf16[224,2560]{1,0:T(8,128)(2,1)} %copy-done.6, bf16[224,2560]{1,0:T(8,128)(2,1)} %collective-permute-done.33.refs_3_, bf16[8,112,2560]{2,1,0:T(8,128)(2,1)} %down.1.refs_0_.refs_4_, ...), custom_call_target="tpu_custom_call" | custom-call | flops 1 | bytes 1 | tf_op jit(solution)/shard_map/hold/pallas_call | solution.py:91
  198.7 3.3 %collective-permute-start.34 = (bf16[448,2560]{1,0:T(8,128)(2,1)}, bf16[448,2560]{1,0:T(8,128)(2,1)}, u32[]{:S(2)}, u32[]{:S(2)}) collective-permute-start(bf16[448,2560]{1,0:T(8,128)(2,1)} %hold.5), channel_id=1, source_target_pairs={{0,1},{1,0},{8,9},{9,8},{16,17},{17,16},{24,25},{25,24},{2,3},{3,2... | collective-permute-start | bytes 6881288 | tf_op jit(solution)/shard_map/ppermute | solution.py:34
  202.1 4.4 %collective-permute-done.34.refs_4_ = bf16[448,2560]{1,0:T(8,128)(2,1)} collective-permute-done((bf16[448,2560]{1,0:T(8,128)(2,1)}, bf16[448,2560]{1,0:T(8,128)(2,1)}, u32[]{:S(2)}, u32[]{:S(2)}) %collective-permute-start.34) | collective-permute-done | bytes 2293792 | tf_op jit(solution)/shard_map/ppermute | solution.py:34
  206.5 8.7 %grad.1 = (bf16[192,2560]{1,0:T(8,128)(2,1)}, bf16[192,2560]{1,0:T(8,128)(2,1)}, bf16[192,2560]{1,0:T(8,128)(2,1)}, bf16[192,2560]{1,0:T(8,128)(2,1)}) custom-call(s32[4]{0:T(128)} %pad_add_fusion.1.refs_0_.where, bf16[896,768]{1,0:T(8,128)(2,1)} %get-tuple-element.86.hidden, bf16[224,2560]{1,0:T(8,128)(2,1)} %get-tuple-element.87.refs_0_, ...), custom_call_target="tpu_custom_call" | custom-call | tf_op jit(solution)/shard_map/grad/pallas_call | solution.py:331
  215.2 1.2 collective-permute-start.35
  216.4 2.4 collective-permute-start.36
  218.8 1.2 collective-permute-start.37
  220.0 15.9 %all-to-all-done.1.rows.refs_0_ = bf16[8,112,2560]{2,1,0:T(8,128)(2,1)} async-done(((bf16[8,112,2560]{2,1,0:T(8,128)(2,1)}), bf16[8,112,2560]{2,1,0:T(8,128)(2,1)}, u32[]{:S(2)}, u32[]{:S(2)}) %all-to-all-start.1) | async-done | bytes 4587552 | tf_op jit(solution)/shard_map/all_to_all | solution.py:410
  235.9 9.0 %combine.1 = (f32[128,2560]{1,0:T(8,128)}, bf16[128,2560]{1,0:T(8,128)(2,1)}, bf16[128,2560]{1,0:T(8,128)(2,1)}, bf16[128,2560]{1,0:T(8,128)(2,1)}) custom-call(f32[16,512]{1,0:T(8,128)} %copy-done, f32[16,512]{1,0:T(8,128)} %copy-done.1, bf16[8,112,2560]{2,1,0:T(8,128)(2,1)} %all-to-all-done.1.rows.refs_0_), custom_call_target="tpu_custom_call" | custom-call | tf_op jit(solution)/shard_map/combine/pallas_call | solution.py:379
  244.9 2.1 collective-permute-start.26
  247.1 14.6 %collective-permute-done.36.c = bf16[192,2560]{1,0:T(8,128)(2,1)} collective-permute-done((bf16[192,2560]{1,0:T(8,128)(2,1)}, bf16[192,2560]{1,0:T(8,128)(2,1)}, u32[]{:S(2)}, u32[]{:S(2)}) %collective-permute-start.36) | collective-permute-done | bytes 983072 | tf_op jit(solution)/shard_map/ppermute | solution.py:34
  261.7 3.5 %sum.1 = bf16[192,2560]{1,0:T(8,128)(2,1)} custom-call(bf16[192,2560]{1,0:T(8,128)(2,1)} %get-tuple-element.90.a, bf16[192,2560]{1,0:T(8,128)(2,1)} %collective-permute-done.35.b, bf16[192,2560]{1,0:T(8,128)(2,1)} %collective-permute-done.36.c, bf16[192,2560]{1,0:T(8,128)(2,1)} %collective-permute-done.37.d, bf16[8,112,2560]{2,1,0:T(8,128)(2,1)} %all-to-all-done.1.rows.refs_0_), custom_call_target="tpu_custom_call" | custom-call | flops 1 | bytes 1 | tf_op jit(solution)/shard_map/sum/pallas_call | solution.py:134
  265.2 1.2 collective-permute-start.38
  266.4 2.1 collective-permute-done.30.other
  268.5 1.2 copy-done.10
  269.7 3.3 %choose.7 = bf16[288,2560]{1,0:T(8,128)(2,1)} custom-call(s32[1]{0:T(128)S(6)} %select_n.115.wanted, bf16[288,2560]{1,0:T(8,128)(2,1)} %copy-done.10, bf16[288,2560]{1,0:T(8,128)(2,1)} %choose.6.own.refs_5_, bf16[8,112,2560]{2,1,0:T(8,128)(2,1)} %down.1.refs_0_.refs_4_), custom_call_target="tpu_custom_call" | custom-call | flops 1 | bytes 1 | tf_op jit(solution)/shard_map/choose/pallas_call | solution.py:114
  273.1 0.8 collective-permute-start.28
  273.9 2.1 add_convert_fusion.1
  275.9 0.7 collective-permute-start.27
  276.8 35.5 %conditional.4 = (bf16[96,2560]{1,0:T(8,128)(2,1)S(1)}, bf16[96,2560]{1,0:T(8,128)(2,1)}) conditional(s32[]{:T(128)} %clamp.3, (bf16[96,2560]{1,0:T(8,128)(2,1)S(1)}, bf16[96,2560]{1,0:T(8,128)(2,1)S(1)}) %tuple.74, (bf16[96,2560]{1,0:T(8,128)(2,1)S(1)}, bf16[96,2560]{1,0:T(8,128)(2,1)S(1)}) %fusion.12, ...), branch_computations={%region_1.2_spmd, %region_2.3_spmd, %region_3.4_spmd, %region_4.5_... | conditional | bytes 4915296
  276.9 3.1 collective-permute-start.11
  280.0 0.8 collective-permute-start.12
  280.8 23.7 %collective-permute-done.11 = bf16[96,2560]{1,0:T(8,128)(2,1)S(1)} collective-permute-done((bf16[96,2560]{1,0:T(8,128)(2,1)S(1)}, bf16[96,2560]{1,0:T(8,128)(2,1)S(1)}, u32[]{:S(2)}, u32[]{:S(2)}) %collective-permute-start.11) | collective-permute-done | bytes 491552 | tf_op jit(solution)/shard_map/cond/branch_6_fun/ppermute | solution.py:34
  304.6 7.8 %collective-permute-done.12 = bf16[96,2560]{1,0:T(8,128)(2,1)} collective-permute-done((bf16[96,2560]{1,0:T(8,128)(2,1)S(1)}, bf16[96,2560]{1,0:T(8,128)(2,1)}, u32[]{:S(2)}, u32[]{:S(2)}) %collective-permute-start.12) | collective-permute-done | bytes 491552 | tf_op jit(solution)/shard_map/cond/branch_6_fun/ppermute | solution.py:34
  312.3 2.9 fusion.4
  315.2 1.1 add_convert_fusion
  (69 shorter events, 1.4 us)
Async XLA Ops:
  7.2 149.4 %all-gather.3.cloned.1.call-start = ((), (), s32[]{:S(2)}) async-start(), calls=%async_computation.2 | async-start | bytes 4423680 | tf_op jit(solution)/shard_map/all_gather | solution.py:482
  7.9 4.7 %copy-start.13 = (bf16[128,2560]{1,0:T(8,128)(2,1)S(1)}, bf16[128,2560]{1,0:T(8,128)(2,1)}, u32[]{:S(2)}) copy-start(bf16[128,2560]{1,0:T(8,128)(2,1)} %refs_2_.1) | copy-start | bytes 1966084
  7.9 36.4 %copy-start.19 = (s32[128,6]{0,1:T(8,128)S(1)}, s32[128,6]{0,1:T(8,128)}, u32[]{:S(2)}) copy-start(s32[128,6]{0,1:T(8,128)} %param.20) | copy-start | bytes 9220
  7.9 36.4 %copy-start.18 = (f32[128,6]{0,1:T(8,128)S(1)}, f32[128,6]{0,1:T(8,128)}, u32[]{:S(2)}) copy-start(f32[128,6]{0,1:T(8,128)} %param.21) | copy-start | bytes 9220
  7.9 47.1 %copy-start.20 = (s32[32]{0:T(128)S(1)}, s32[32]{0:T(128)}, u32[]{:S(2)}) copy-start(s32[32]{0:T(128)} %param.22) | copy-start | bytes 388
  10.5 46.8 %collective-permute-start.21 = (bf16[288,2560]{1,0:T(8,128)(2,1)}, bf16[288,2560]{1,0:T(8,128)(2,1)S(1)}, u32[]{:S(2)}, u32[]{:S(2)}) collective-permute-start(bf16[288,2560]{1,0:T(8,128)(2,1)} %hold.3.own), channel_id=1, source_target_pairs={{0,8},{1,9},{8,0},{9,1},{16,24},{17,25},{24,16},{25,17},{2,10},{3,... | collective-permute-start | bytes 4423688 | tf_op jit(solution)/shard_map/ppermute | solution.py:34
  12.6 27.9 %collective-permute-start.18 = (bf16[128,2560]{1,0:T(8,128)(2,1)S(1)}, bf16[128,2560]{1,0:T(8,128)(2,1)S(1)}, u32[]{:S(2)}, u32[]{:S(2)}) collective-permute-start(bf16[128,2560]{1,0:T(8,128)(2,1)S(1)} %copy-done.13), channel_id=1, source_target_pairs={{0,2},{1,39},{8,10},{9,47},{16,18},{17,55},{24,26},{25,63},{2,4},{... | collective-permute-start | bytes 1966088 | tf_op jit(solution)/shard_map/ppermute | solution.py:34
  18.2 39.1 %collective-permute-start.19 = (bf16[128,2560]{1,0:T(8,128)(2,1)S(1)}, bf16[128,2560]{1,0:T(8,128)(2,1)S(1)}, u32[]{:S(2)}, u32[]{:S(2)}) collective-permute-start(bf16[128,2560]{1,0:T(8,128)(2,1)S(1)} %copy-done.13), channel_id=1, source_target_pairs={{0,38},{1,3},{8,46},{9,11},{16,54},{17,19},{24,62},{25,27},{2,0},{... | collective-permute-start | bytes 1966088 | tf_op jit(solution)/shard_map/ppermute | solution.py:34
  40.5 16.9 %copy-start.14 = (bf16[128,2560]{1,0:T(8,128)(2,1)}, bf16[128,2560]{1,0:T(8,128)(2,1)S(1)}, u32[]{:S(2)}) copy-start(bf16[128,2560]{1,0:T(8,128)(2,1)S(1)} %collective-permute-done.18.refs_3_) | copy-start | bytes 1966084
  40.5 16.8 %collective-permute-start.20 = (bf16[128,2560]{1,0:T(8,128)(2,1)S(1)}, bf16[128,2560]{1,0:T(8,128)(2,1)}, u32[]{:S(2)}, u32[]{:S(2)}) collective-permute-start(bf16[128,2560]{1,0:T(8,128)(2,1)S(1)} %collective-permute-done.18.refs_3_), channel_id=1, source_target_pairs={{0,2},{1,39},{8,10},{9,47},{16,18},{17,55},{24,26},{25,63},{2,4},{... | collective-permute-start | bytes 1966088 | tf_op jit(solution)/shard_map/ppermute | solution.py:34
  44.3 7.6 %collective-permute-start.15 = (f32[16,128]{1,0:T(8,128)S(1)}, f32[16,128]{1,0:T(8,128)S(1)}, u32[]{:S(2)}, u32[]{:S(2)}) collective-permute-start(f32[16,128]{1,0:T(8,128)S(1)} %pad_maximum_fusion.refs_1_), channel_id=1, source_target_pairs={{0,2},{1,39},{8,10},{9,47},{16,18},{17,55},{24,26},{25,63},{2,4},{... | collective-permute-start | bytes 24584 | tf_op jit(solution)/shard_map/ppermute | solution.py:34
  44.4 10.8 %collective-permute-start.16 = (f32[16,128]{1,0:T(8,128)S(1)}, f32[16,128]{1,0:T(8,128)S(1)}, u32[]{:S(2)}, u32[]{:S(2)}) collective-permute-start(f32[16,128]{1,0:T(8,128)S(1)} %pad_maximum_fusion.refs_1_), channel_id=1, source_target_pairs={{0,38},{1,3},{8,46},{9,11},{16,54},{17,19},{24,62},{25,27},{2,0},{... | collective-permute-start | bytes 24584 | tf_op jit(solution)/shard_map/ppermute | solution.py:34
  51.9 3.9 %collective-permute-start.17 = (f32[16,128]{1,0:T(8,128)S(1)}, f32[16,128]{1,0:T(8,128)S(1)}, u32[]{:S(2)}, u32[]{:S(2)}) collective-permute-start(f32[16,128]{1,0:T(8,128)S(1)} %collective-permute-done.15.refs_2_), channel_id=1, source_target_pairs={{0,2},{1,39},{8,10},{9,47},{16,18},{17,55},{24,26},{25,63},{2,4},{... | collective-permute-start | bytes 24584 | tf_op jit(solution)/shard_map/ppermute | solution.py:34
  56.1 0.6 copy-start
  56.7 0.6 copy-start.1
  57.3 0.8 copy-start.15
  57.3 1.3 copy-start.3
  65.8 64.1 %all-to-all-start = ((bf16[8,112,2560]{2,1,0:T(8,128)(2,1)}), bf16[8,112,2560]{2,1,0:T(8,128)(2,1)}, u32[]{:S(2)}, u32[]{:S(2)}) async-start(bf16[8,112,2560]{2,1,0:T(8,128)(2,1)} %select.92.refs_1_.refs_0_), calls=%async_computation | async-start | bytes 9175040 | tf_op jit(solution)/shard_map/all_to_all | solution.py:410
  76.7 45.3 %collective-permute-start.25 = (bf16[288,2560]{1,0:T(8,128)(2,1)}, bf16[288,2560]{1,0:T(8,128)(2,1)S(1)}, u32[]{:S(2)}, u32[]{:S(2)}) collective-permute-start(bf16[288,2560]{1,0:T(8,128)(2,1)} %choose.4.own), channel_id=1, source_target_pairs={{0,1},{1,0},{8,9},{9,8},{16,17},{17,16},{24,25},{25,24},{2,3},{3,2... | collective-permute-start | bytes 4423688 | tf_op jit(solution)/shard_map/ppermute | solution.py:34
  78.8 40.6 %collective-permute-start.22 = (bf16[128,2560]{1,0:T(8,128)(2,1)}, bf16[128,2560]{1,0:T(8,128)(2,1)S(1)}, u32[]{:S(2)}, u32[]{:S(2)}) collective-permute-start(bf16[128,2560]{1,0:T(8,128)(2,1)} %hold.4.refs_2_), channel_id=1, source_target_pairs={{0,2},{1,39},{8,10},{9,47},{16,18},{17,55},{24,26},{25,63},{2,4},{... | collective-permute-start | bytes 1966088 | tf_op jit(solution)/shard_map/ppermute | solution.py:34
  79.1 42.9 %collective-permute-start.23 = (bf16[128,2560]{1,0:T(8,128)(2,1)}, bf16[128,2560]{1,0:T(8,128)(2,1)S(1)}, u32[]{:S(2)}, u32[]{:S(2)}) collective-permute-start(bf16[128,2560]{1,0:T(8,128)(2,1)} %hold.4.refs_2_), channel_id=1, source_target_pairs={{0,38},{1,3},{8,46},{9,11},{16,54},{17,19},{24,62},{25,27},{2,0},{... | collective-permute-start | bytes 1966088 | tf_op jit(solution)/shard_map/ppermute | solution.py:34
  119.4 2.6 copy-start.8
  119.4 10.5 %collective-permute-start.24 = (bf16[128,2560]{1,0:T(8,128)(2,1)S(1)}, bf16[128,2560]{1,0:T(8,128)(2,1)S(1)}, u32[]{:S(2)}, u32[]{:S(2)}) collective-permute-start(bf16[128,2560]{1,0:T(8,128)(2,1)S(1)} %collective-permute-done.22.refs_0_.refs_3_), channel_id=1, source_target_pairs={{0,2},{1,39},{8,10},{9,47},{16,18},{17,55},{24,26},{25,63},{2,4},{... | collective-permute-start | bytes 1966088 | tf_op jit(solution)/shard_map/ppermute | solution.py:34
  122.0 0.9 copy-start.9
  122.9 1.1 copy-start.11
  127.0 47.5 %collective-permute-start.29 = (bf16[288,2560]{1,0:T(8,128)(2,1)}, bf16[288,2560]{1,0:T(8,128)(2,1)}, u32[]{:S(2)}, u32[]{:S(2)}) collective-permute-start(bf16[288,2560]{1,0:T(8,128)(2,1)} %choose.5.refs_7_.own), channel_id=1, source_target_pairs={{0,2},{1,3},{8,10},{9,11},{16,18},{17,19},{24,26},{25,27},{2,0},{3... | collective-permute-start | bytes 4423688 | tf_op jit(solution)/shard_map/ppermute | solution.py:34
  129.8 0.8 copy-start.16
  137.4 40.2 %collective-permute-start.31 = (bf16[224,2560]{1,0:T(8,128)(2,1)}, bf16[224,2560]{1,0:T(8,128)(2,1)S(1)}, u32[]{:S(2)}, u32[]{:S(2)}) collective-permute-start(bf16[224,2560]{1,0:T(8,128)(2,1)} %get-tuple-element.88), channel_id=1, source_target_pairs={{0,8},{1,9},{8,16},{9,17},{16,24},{17,25},{24,0},{25,1},{2,10},{3,... | collective-permute-start | bytes 3440648 | tf_op jit(solution)/shard_map/ppermute | solution.py:34
  138.6 48.1 %collective-permute-start.32 = (bf16[224,2560]{1,0:T(8,128)(2,1)}, bf16[224,2560]{1,0:T(8,128)(2,1)S(1)}, u32[]{:S(2)}, u32[]{:S(2)}) collective-permute-start(bf16[224,2560]{1,0:T(8,128)(2,1)} %get-tuple-element.89), channel_id=1, source_target_pairs={{0,16},{1,17},{8,24},{9,25},{16,0},{17,1},{24,8},{25,9},{2,18},{3,... | collective-permute-start | bytes 3440648 | tf_op jit(solution)/shard_map/ppermute | solution.py:34
  141.0 53.8 %collective-permute-start.33 = (bf16[224,2560]{1,0:T(8,128)(2,1)}, bf16[224,2560]{1,0:T(8,128)(2,1)}, u32[]{:S(2)}, u32[]{:S(2)}) collective-permute-start(bf16[224,2560]{1,0:T(8,128)(2,1)} %get-tuple-element.80.refs_4_), channel_id=1, source_target_pairs={{0,24},{1,25},{8,0},{9,1},{16,8},{17,9},{24,16},{25,17},{2,26},{3,... | collective-permute-start | bytes 3440648 | tf_op jit(solution)/shard_map/ppermute | solution.py:34
  164.7 71.2 %all-to-all-start.1 = ((bf16[8,112,2560]{2,1,0:T(8,128)(2,1)}), bf16[8,112,2560]{2,1,0:T(8,128)(2,1)}, u32[]{:S(2)}, u32[]{:S(2)}) async-start(bf16[8,112,2560]{2,1,0:T(8,128)(2,1)} %down.1.refs_0_.refs_4_), calls=%async_computation.1 | async-start | bytes 9175040 | tf_op jit(solution)/shard_map/all_to_all | solution.py:410
  177.6 17.2 %copy-start.5 = (bf16[224,2560]{1,0:T(8,128)(2,1)}, bf16[224,2560]{1,0:T(8,128)(2,1)S(1)}, u32[]{:S(2)}) copy-start(bf16[224,2560]{1,0:T(8,128)(2,1)S(1)} %collective-permute-done.31.refs_1_) | copy-start | bytes 3440644
  186.7 8.1 %copy-start.6 = (bf16[224,2560]{1,0:T(8,128)(2,1)}, bf16[224,2560]{1,0:T(8,128)(2,1)S(1)}, u32[]{:S(2)}) copy-start(bf16[224,2560]{1,0:T(8,128)(2,1)S(1)} %collective-permute-done.32.refs_2_) | copy-start | bytes 3440644
  194.8 7.3 %copy-start.2 = (bf16[288,2560]{1,0:T(8,128)(2,1)S(1)}, bf16[288,2560]{1,0:T(8,128)(2,1)}, u32[]{:S(2)}) copy-start(bf16[288,2560]{1,0:T(8,128)(2,1)} %choose.6.own.refs_5_) | copy-start | bytes 4423684
  198.7 7.7 %collective-permute-start.34 = (bf16[448,2560]{1,0:T(8,128)(2,1)}, bf16[448,2560]{1,0:T(8,128)(2,1)}, u32[]{:S(2)}, u32[]{:S(2)}) collective-permute-start(bf16[448,2560]{1,0:T(8,128)(2,1)} %hold.5), channel_id=1, source_target_pairs={{0,1},{1,0},{8,9},{9,8},{16,17},{17,16},{24,25},{25,24},{2,3},{3,2... | collective-permute-start | bytes 6881288 | tf_op jit(solution)/shard_map/ppermute | solution.py:34
  202.1 66.5 %collective-permute-start.30 = (bf16[288,2560]{1,0:T(8,128)(2,1)S(1)}, bf16[288,2560]{1,0:T(8,128)(2,1)S(1)}, u32[]{:S(2)}, u32[]{:S(2)}) collective-permute-start(bf16[288,2560]{1,0:T(8,128)(2,1)S(1)} %copy-done.2), channel_id=1, source_target_pairs={{0,4},{1,5},{8,12},{9,13},{16,20},{17,21},{24,28},{25,29},{2,6},{3... | collective-permute-start | bytes 4423688 | tf_op jit(solution)/shard_map/ppermute | solution.py:34
  215.2 31.8 %collective-permute-start.35 = (bf16[192,2560]{1,0:T(8,128)(2,1)}, bf16[192,2560]{1,0:T(8,128)(2,1)}, u32[]{:S(2)}, u32[]{:S(2)}) collective-permute-start(bf16[192,2560]{1,0:T(8,128)(2,1)} %get-tuple-element.91), channel_id=1, source_target_pairs={{0,64},{1,65},{8,72},{9,73},{16,80},{17,81},{24,88},{25,89},{2,66}... | collective-permute-start | bytes 2949128 | tf_op jit(solution)/shard_map/ppermute | solution.py:34
  216.4 45.3 %collective-permute-start.36 = (bf16[192,2560]{1,0:T(8,128)(2,1)}, bf16[192,2560]{1,0:T(8,128)(2,1)}, u32[]{:S(2)}, u32[]{:S(2)}) collective-permute-start(bf16[192,2560]{1,0:T(8,128)(2,1)} %get-tuple-element.92), channel_id=1, source_target_pairs={{0,128},{1,129},{8,136},{9,137},{16,144},{17,145},{24,152},{25,153... | collective-permute-start | bytes 2949128 | tf_op jit(solution)/shard_map/ppermute | solution.py:34
  218.8 42.9 %collective-permute-start.37 = (bf16[192,2560]{1,0:T(8,128)(2,1)}, bf16[192,2560]{1,0:T(8,128)(2,1)}, u32[]{:S(2)}, u32[]{:S(2)}) collective-permute-start(bf16[192,2560]{1,0:T(8,128)(2,1)} %get-tuple-element.93), channel_id=1, source_target_pairs={{0,192},{1,193},{8,200},{9,201},{16,208},{17,209},{24,216},{25,217... | collective-permute-start | bytes 2949128 | tf_op jit(solution)/shard_map/ppermute | solution.py:34
  244.9 29.0 %collective-permute-start.26 = (bf16[128,2560]{1,0:T(8,128)(2,1)}, bf16[128,2560]{1,0:T(8,128)(2,1)}, u32[]{:S(2)}, u32[]{:S(2)}) collective-permute-start(bf16[128,2560]{1,0:T(8,128)(2,1)} %get-tuple-element.83), channel_id=1, source_target_pairs={{0,38},{1,3},{8,46},{9,11},{16,54},{17,19},{24,62},{25,27},{2,0},{... | collective-permute-start | bytes 1966088 | tf_op jit(solution)/shard_map/ppermute | solution.py:34
  265.2 11.4 %collective-permute-start.38 = (bf16[192,2560]{1,0:T(8,128)(2,1)}, bf16[192,2560]{1,0:T(8,128)(2,1)}, u32[]{:S(2)}, u32[]{:S(2)}) collective-permute-start(bf16[192,2560]{1,0:T(8,128)(2,1)} %sum.1), channel_id=1, source_target_pairs={{0,1},{1,0},{8,9},{9,8},{16,17},{17,16},{24,25},{25,24},{2,3},{3,2... | collective-permute-start | bytes 2949128 | tf_op jit(solution)/shard_map/ppermute | solution.py:34
  268.5 1.2 copy-start.10
  269.7 4.2 %copy-start.17 = (bf16[128,2560]{1,0:T(8,128)(2,1)S(1)}, bf16[128,2560]{1,0:T(8,128)(2,1)}, u32[]{:S(2)}) copy-start(bf16[128,2560]{1,0:T(8,128)(2,1)} %get-tuple-element.84) | copy-start | bytes 1966084
  273.1 3.6 %copy-start.7 = (bf16[192,2560]{1,0:T(8,128)(2,1)S(1)}, bf16[192,2560]{1,0:T(8,128)(2,1)}, u32[]{:S(2)}) copy-start(bf16[192,2560]{1,0:T(8,128)(2,1)} %sum.1) | copy-start | bytes 2949124
  273.1 42.2 %collective-permute-start.28 = (bf16[128,2560]{1,0:T(8,128)(2,1)}, bf16[128,2560]{1,0:T(8,128)(2,1)S(1)}, u32[]{:S(2)}, u32[]{:S(2)}) collective-permute-start(bf16[128,2560]{1,0:T(8,128)(2,1)} %get-tuple-element.85), channel_id=1, source_target_pairs={{0,2},{1,39},{8,10},{9,47},{16,18},{17,55},{24,26},{25,63},{2,4},{... | collective-permute-start | bytes 1966088 | tf_op jit(solution)/shard_map/ppermute | solution.py:34
  275.9 39.3 %collective-permute-start.27 = (bf16[128,2560]{1,0:T(8,128)(2,1)}, bf16[128,2560]{1,0:T(8,128)(2,1)S(1)}, u32[]{:S(2)}, u32[]{:S(2)}) collective-permute-start(bf16[128,2560]{1,0:T(8,128)(2,1)} %add_convert_fusion.1), channel_id=1, source_target_pairs={{0,38},{1,3},{8,46},{9,11},{16,54},{17,19},{24,62},{25,27},{2,0},{... | collective-permute-start | bytes 1966088 | tf_op jit(solution)/shard_map/ppermute | solution.py:34
  276.8 35.5 %copy-start.4 = (bf16[288,2560]{1,0:T(8,128)(2,1)S(1)}, bf16[288,2560]{1,0:T(8,128)(2,1)}, u32[]{:S(2)}) copy-start(bf16[288,2560]{1,0:T(8,128)(2,1)} %choose.7) | copy-start | bytes 4423684
  276.9 27.7 %collective-permute-start.11 = (bf16[96,2560]{1,0:T(8,128)(2,1)S(1)}, bf16[96,2560]{1,0:T(8,128)(2,1)S(1)}, u32[]{:S(2)}, u32[]{:S(2)}) collective-permute-start(bf16[96,2560]{1,0:T(8,128)(2,1)S(1)} %get-tuple-element.52), channel_id=1, source_target_pairs={{0,12},{1,13},{8,4},{9,5},{16,28},{17,29},{24,20},{25,21},{2,14},{... | collective-permute-start | bytes 1474568 | tf_op jit(solution)/shard_map/cond/branch_6_fun/ppermute | solution.py:34
  280.0 32.4 %collective-permute-start.12 = (bf16[96,2560]{1,0:T(8,128)(2,1)S(1)}, bf16[96,2560]{1,0:T(8,128)(2,1)}, u32[]{:S(2)}, u32[]{:S(2)}) collective-permute-start(bf16[96,2560]{1,0:T(8,128)(2,1)S(1)} %get-tuple-element.53), channel_id=1, source_target_pairs={{0,44},{1,45},{8,36},{9,37},{16,60},{17,61},{24,52},{25,53},{2,46}... | collective-permute-start | bytes 1474568 | tf_op jit(solution)/shard_map/cond/branch_6_fun/ppermute | solution.py:34
  312.3 2.9 copy-start.12
Sparse Core Ops, SparseCore 0:
  10.6 109.3 all-gather.2
where the time goes:
time: 325 us; the launch traced here: 323 us
  waiting for transfers between devices  158 us (49%)
  Pallas kernels  78.3 us (24%)
  starting transfers between devices  57.9 us (18%)
  between operations  14.9 us (5%)
  other arithmetic  7.05 us (2%)
  local copies, waits for them, and re-layouts  6.73 us (2%)
    ppermute x26, waiting for transfers between devices, permute(): return lax.ppermute(array, AXES, pairs)  142 us
    ppermute x26, starting transfers between devices, permute(): return lax.ppermute(array, AXES, pairs)  40.9 us
    all_to_all x2, starting transfers between devices, plane_exchange(): lax.all_to_all(rows, ('x', 'c'), split_axis=0, concat_axis=0, tiled=True)  16.9 us
    all_to_all x2, waiting for transfers between devices, plane_exchange(): lax.all_to_all(rows, ('x', 'c'), split_axis=0, concat_axis=0, tiled=True)  15.9 us
    pallas_call x2, Pallas kernels, select_rows(): pl.pallas_call(lambda *refs: select_kernel(scaled, *refs), grid=(width //...  13.8 us
    pallas_call x1, Pallas kernels, hidden_rows(): pl.pallas_call(lambda *refs: hidden_kernel(len(xs), *refs), grid=(steps,)...  13.8 us
    pallas_call x4, Pallas kernels, choose(): pl.pallas_call(choose_kernel, in_specs=[pl.BlockSpec(memory_space=pltpu.S...  12.5 us
    pallas_call x1, Pallas kernels, combine_rows(): pl.pallas_call(combine_kernel, grid=(width // tile,), in_specs=[whole, wh...  8.99 us
  transfers between devices with their start and end apart: 29, of which 14 were waited for; matrix products, arithmetic and copies ran while one was open for 2% of the time, Pallas kernels for 24%

commit v1 on v0

--- a/solution.py
+++ b/solution.py
@@ -15,8 +15,8 @@
 learn_rate = 0.003
 adam_eps = 1e-08
 
-G_CHUNKS = 1
-R_CHUNKS = 1
+G_CHUNKS = 2
+R_CHUNKS = 2
 
 
 def flat_index(y, z, x, c):
@@ -100,6 +100,32 @@
     )(*arrays, *earlier)
 
 
+def mark_kernel(tokens, meta, out):
+    width = tokens.shape[1]
+    out[:, :width] = tokens[...]
+    left = meta[...]
+    total = None
+    for turn in range(3):
+        part = left.astype(jnp.bfloat16).astype(jnp.float32)
+        left = left - part
+        part = pltpu.roll(part, 16 * turn, 1) if turn else part
+        total = part if total is None else total + part
+    out[:, width:] = total.astype(jnp.bfloat16)
+
+
+def mark(tokens, meta):
+    rows, width = tokens.shape
+    return pl.pallas_call(
+        mark_kernel,
+        in_specs=[pl.BlockSpec(memory_space=pltpu.VMEM)] * 2,
+        out_specs=pl.BlockSpec(memory_space=pltpu.VMEM),
+        out_shape=jax.ShapeDtypeStruct((rows, width + 128), jnp.bfloat16),
+        compiler_params=params(60),
+        cost_estimate=LIGHT,
+        name="mark",
+    )(tokens, meta)
+
+
 def choose_kernel(wanted, other, own, *refs):
     @pl.when(wanted[0] == 1)
     def _():
@@ -124,53 +150,43 @@
     )(wanted, other, own, *earlier)
 
 
-def sum_kernel(a, b, c, d, *refs):
-    total = a[...].astype(jnp.float32) + b[...].astype(jnp.float32)
-    total = total + c[...].astype(jnp.float32) + d[...].astype(jnp.float32)
-    refs[-1][...] = total.astype(jnp.bfloat16)
-
-
-def sum_blocks(blocks, *earlier):
-    return pl.pallas_call(
-        sum_kernel,
-        in_specs=[pl.BlockSpec(memory_space=pltpu.VMEM) for _ in blocks]
-        + [pl.BlockSpec(memory_space=pl.ANY) for _ in earlier],
-        out_specs=pl.BlockSpec(memory_space=pltpu.VMEM),
-        out_shape=jax.ShapeDtypeStruct(blocks[0].shape, jnp.bfloat16),
-        compiler_params=params(60),
-        cost_estimate=LIGHT,
-        name="sum",
-    )(*blocks, *earlier)
-
-
 def plan_kernel(cap, top, ids_here, m0, m1, m2, m3, slot_ref, weight_ref):
-    rows = m0.shape[1]
+    rows = m0.shape[0]
     before = lax.broadcasted_iota(jnp.int32, (rows, rows), 0)
     after = lax.broadcasted_iota(jnp.int32, (rows, rows), 1)
     earlier = (before < after).astype(jnp.float32).astype(jnp.bfloat16)
     wanted = ids_here[...]
-    for s, meta in enumerate((m0, m1, m2, m3)):
+    for s, block in enumerate((m0, m1, m2, m3)):
+        meta = block[...].astype(jnp.float32).T
+        scale = meta[8:16, :] + meta[24:32, :] + meta[40:48, :]
         named = jnp.zeros(wanted.shape, jnp.float32)
         weight = jnp.zeros(wanted.shape, jnp.float32)
         for k in range(top):
             same = (meta[k : k + 1, :] == wanted).astype(jnp.float32)
             named = named + same
-            weight = weight + same * meta[8 + k : 9 + k, :]
+            weight = weight + same * scale[k : k + 1, :]
         rank = jnp.dot(named.astype(jnp.bfloat16), earlier, preferred_element_type=jnp.float32)
         slot = jnp.where(named > 0.5, rank + float(s * cap), -1.0)
         slot_ref[:, s * rows : (s + 1) * rows] = slot
         weight_ref[:, s * rows : (s + 1) * rows] = weight
 
 
-def make_plan(cap, top, ids_here, metas):
-    rows = metas[0].shape[1]
+def make_plan(cap, top, ids_here, parts):
+    rows, width = parts[0].shape
+    last = width // 128 - 1
     out = jax.ShapeDtypeStruct((ids_here.shape[0], 4 * rows), jnp.float32)
+    whole = pl.BlockSpec(out.shape, lambda i: (0, 0))
     return pl.pallas_call(
         lambda *refs: plan_kernel(cap, top, *refs),
+        grid=(1,),
+        in_specs=[pl.BlockSpec(ids_here.shape, lambda i: (0, 0))]
+        + [pl.BlockSpec((rows, 128), lambda i: (0, last)) for _ in parts],
+        out_specs=(whole, whole),
         out_shape=(out, out),
-        compiler_params=params(16),
+        compiler_params=params(60, "arbitrary"),
+        cost_estimate=LIGHT,
         name="plan",
-    )(ids_here, *metas)
+    )(ids_here, *parts)
 
 
 def select_kernel(scaled, slots, weights, t0, t1, t2, t3, *refs):
@@ -199,11 +215,12 @@
         outs[-1][...] = rows.astype(jnp.bfloat16).reshape(8, block, -1)
 
 
-def select_rows(scaled, cap, plan, parts, *earlier):
+def select_rows(scaled, cap, plan, parts, first, width, *earlier):
     slots, weights = plan
-    rows, width = parts[0].shape
+    rows = parts[0].shape[0]
     block = 4 * cap
-    tile = 512
+    tile = 256 if width % 512 else 512
+    offset = first // tile
     whole = pl.BlockSpec(slots.shape, lambda j: (0, 0))
     if scaled:
         out_spec = (pl.BlockSpec((2 * block, tile), lambda j: (0, j)),) * 4
@@ -215,7 +232,7 @@
         lambda *refs: select_kernel(scaled, *refs),
         grid=(width // tile,),
         in_specs=[whole, whole]
-        + [pl.BlockSpec((rows, tile), lambda j: (0, j)) for _ in range(4)]
+        + [pl.BlockSpec((rows, tile), lambda j: (0, j + offset)) for _ in range(4)]
         + [pl.BlockSpec(memory_space=pl.ANY) for _ in earlier],
         out_specs=out_spec,
         out_shape=out_shape,
@@ -229,10 +246,8 @@
     )(slots, weights, *parts, *earlier)
 
 
-def hidden_kernel(count, where, *refs):
-    xs, (gate_w, up_w, _, fixed, turned, held) = refs[:count], refs[count:]
-    step, tile = pl.program_id(0), gate_w.shape[1]
-    steps, features = held.shape[0], fixed.shape[1]
+def hidden_kernel(count, *refs):
+    xs, (gate_w, up_w), out = refs[:count], refs[count : count + 2], refs[-1]
     gate, up, first = None, None, 0
     for x in xs:
         rows = x[...].reshape(-1, x.shape[2])
@@ -241,52 +256,34 @@
         g = jnp.dot(rows, gate_w[part, :], preferred_element_type=jnp.float32)
         u = jnp.dot(rows, up_w[part, :], preferred_element_type=jnp.float32)
         gate, up = (g, u) if gate is None else (gate + g, up + u)
-    held[step] = (gate / (1.0 + jnp.exp(-gate)) * up).astype(jnp.bfloat16)
-
-    @pl.when(step == steps - 1)
-    def _():
-        shard = features // (N_Y * N_ZH)
-        column = lax.broadcasted_iota(jnp.int32, (tile, features), 1)
-        row = lax.broadcasted_iota(jnp.int32, (tile, features), 0)
-        number = column // shard
-        zh = (where[1] + number % 2) % N_ZH
-        y = (where[0] + number // 2) % N_Y
-        origin = (y * N_ZH + zh) * shard + (column - number * shard)
-        total = None
-        for s in range(steps):
-            fixed[:, s * tile : (s + 1) * tile] = held[s]
-            move = (row + s * tile == origin).astype(jnp.float32).astype(jnp.bfloat16)
-            part = jnp.dot(held[s], move, preferred_element_type=jnp.float32)
-            total = part if total is None else total + part
-        turned[...] = total.astype(jnp.bfloat16)
-
-
-def hidden_rows(where, xs, gate_weight, up_weight, earlier):
+    out[...] = (gate / (1.0 + jnp.exp(-gate)) * up).astype(jnp.bfloat16)
+
+
+def hidden_rows(xs, gate_weight, up_weight, earlier):
     depth, features = gate_weight.shape
     count = xs[0].shape[0] * xs[0].shape[1]
     tile = 256
-    steps = features // tile
     return pl.pallas_call(
         lambda *refs: hidden_kernel(len(xs), *refs),
-        grid=(steps,),
-        in_specs=[pl.BlockSpec(memory_space=pltpu.SMEM)]
-        + [pl.BlockSpec(x.shape, lambda j: (0, 0, 0)) for x in xs]
+        grid=(features // tile,),
+        in_specs=[pl.BlockSpec(x.shape, lambda j: (0, 0, 0)) for x in xs]
         + [pl.BlockSpec((depth, tile), lambda j: (0, j)) for _ in range(2)]
-        + [pl.BlockSpec(memory_space=pl.ANY)],
-        out_specs=(pl.BlockSpec((count, features), lambda j: (0, 0)),) * 2,
-        out_shape=(jax.ShapeDtypeStruct((count, features), jnp.bfloat16),) * 2,
-        scratch_shapes=[pltpu.VMEM((steps, count, tile), jnp.bfloat16)],
+        + [pl.BlockSpec(memory_space=pl.ANY) for _ in earlier],
+        out_specs=pl.BlockSpec((count, tile), lambda j: (0, j)),
+        out_shape=jax.ShapeDtypeStruct((count, features), jnp.bfloat16),
         compiler_params=params(60, "arbitrary"),
+        cost_estimate=LIGHT,
         name="hidden",
-    )(where, *xs, gate_weight, up_weight, earlier)
-
-
-def down_kernel(hidden, down, out):
+    )(*xs, gate_weight, up_weight, *earlier)
+
+
+def down_kernel(hidden, down, *refs):
+    out = refs[-1]
     rows = jnp.dot(hidden[...], down[...], preferred_element_type=jnp.float32)
     out[...] = rows.astype(jnp.bfloat16).reshape(out.shape)
 
 
-def down_rows(hidden, down, cap, first, width):
+def down_rows(hidden, down, cap, first, width, *earlier):
     tile = 256 if width % 512 else 512
     offset = first // tile
     block = 4 * cap
@@ -294,40 +291,38 @@
         down_kernel,
         grid=(width // tile,),
         in_specs=[pl.BlockSpec(hidden.shape, lambda j: (0, 0))]
-        + [pl.BlockSpec((down.shape[0], tile), lambda j: (0, j + offset))],
+        + [pl.BlockSpec((down.shape[0], tile), lambda j: (0, j + offset))]
+        + [pl.BlockSpec(memory_space=pl.ANY) for _ in earlier],
         out_specs=pl.BlockSpec((8, block, tile), lambda j: (0, 0, j)),
         out_shape=jax.ShapeDtypeStruct((8, block, width), jnp.bfloat16),
         compiler_params=params(60, "arbitrary"),
+        cost_estimate=LIGHT,
         name="down",
-    )(hidden, down)
+    )(hidden, down, *earlier)
 
 
 def grad_kernel(where, hidden, *refs):
-    rows, outs, turned = refs[:5], refs[5:9], refs[9]
+    rows, out, turned = refs[:5], refs[5], refs[6]
     block = rows[0].shape[0]
 
     @pl.when(pl.program_id(0) == 0)
     def _():
         parts = []
         for k in range(8):
-            source = (where[2] + N_X - k % 4) % N_X * 2 + (where[3] + k // 4) % 2
+            source = (where[0] + N_X - k % 4) % N_X * 2 + (where[1] + k // 4) % 2
             parts.append(hidden[pl.ds(pl.multiple_of(source * block, 16), block), :])
         turned[...] = jnp.concatenate(parts, axis=0).T
 
     value = jnp.concatenate([r[...] for r in rows], axis=0)
-    grad = jnp.dot(turned[...], value, preferred_element_type=jnp.float32).astype(jnp.bfloat16)
-    quarter = outs[0].shape[0]
-    for k, out in enumerate(outs):
-        out[...] = grad[k * quarter : (k + 1) * quarter, :]
-
-
-def grad_blocks(where, hidden, rows, first, width):
+    grad = jnp.dot(turned[...], value, preferred_element_type=jnp.float32)
+    out[...] = grad.astype(jnp.bfloat16)
+
+
+def grad_partial(where, hidden, rows):
+    width = rows[0].shape[1]
     block = rows[0].shape[0] // 2
     tile = 256 if width % 512 else 512
-    offset = first // tile
-    quarter = hidden.shape[1] // N_Y
-    spec = pl.BlockSpec((quarter, tile), lambda j: (0, j))
-    out = jax.ShapeDtypeStruct((quarter, width), jnp.bfloat16)
+    features = hidden.shape[1]
     return pl.pallas_call(
         grad_kernel,
         grid=(width // tile,),
@@ -335,17 +330,19 @@
             pl.BlockSpec(memory_space=pltpu.SMEM),
             pl.BlockSpec(hidden.shape, lambda j: (0, 0)),
         ]
-        + [pl.BlockSpec((block, tile), lambda j: (0, j + offset)) for _ in range(4)]
-        + [pl.BlockSpec((4 * block, tile), lambda j: (0, j + offset))],
-        out_specs=(spec,) * 4,
-        out_shape=(out,) * 4,
+        + [pl.BlockSpec((block, tile), lambda j: (0, j)) for _ in range(4)]
+        + [pl.BlockSpec((4 * block, tile), lambda j: (0, j))],
+        out_specs=pl.BlockSpec((features, tile), lambda j: (0, j)),
+        out_shape=jax.ShapeDtypeStruct((features, width), jnp.bfloat16),
         scratch_shapes=[pltpu.VMEM(hidden.shape[::-1], jnp.bfloat16)],
         compiler_params=params(60, "arbitrary"),
+        cost_estimate=LIGHT,
         name="grad",
     )(where, hidden, *rows)
 
 
-def combine_kernel(slots, weights, rows, o0, o1, o2, o3, high, low):
+def combine_kernel(slots, weights, rows, *refs):
+    *outs, high, low = refs[-6:]
     dests, block, width = rows.shape
     tokens = slots.shape[1]
 
@@ -364,12 +361,12 @@
     value = rows[...].reshape(-1, width)
     total = jnp.dot(high[...], value, preferred_element_type=jnp.float32)
     total = total + jnp.dot(low[...], value, preferred_element_type=jnp.float32)
-    count = o0.shape[0]
-    for s, out in enumerate((o0, o1, o2, o3)):
+    count = outs[0].shape[0]
+    for s, out in enumerate(outs):
         out[...] = total[s * count : (s + 1) * count, :].astype(out.dtype)
 
 
-def combine_rows(plan, rows):
+def combine_rows(plan, rows, *earlier):
     slots, weights = plan
     width = rows.shape[2]
     tile = 256 if width % 512 else 512
@@ -379,7 +376,8 @@
     return pl.pallas_call(
         combine_kernel,
         grid=(width // tile,),
-        in_specs=[whole, whole, pl.BlockSpec((*rows.shape[:2], tile), lambda j: (0, 0, j))],
+        in_specs=[whole, whole, pl.BlockSpec((*rows.shape[:2], tile), lambda j: (0, 0, j))]
+        + [pl.BlockSpec(memory_space=pl.ANY) for _ in earlier],
         out_specs=(spec,) * 4,
         out_shape=tuple(
             jax.ShapeDtypeStruct((count, width), t)
@@ -390,8 +388,9 @@
             for _ in range(2)
         ],
         compiler_params=params(60, "arbitrary"),
+        cost_estimate=LIGHT,
         name="combine",
-    )(slots, weights, rows)
+    )(slots, weights, rows, *earlier)
 
 
 def plane_permute(blocks):
@@ -416,10 +415,6 @@
     from_other = z_up(other)
     total = own + from_near.astype(jnp.float32) + from_other.astype(jnp.float32)
     return total.astype(jnp.bfloat16)
-
-
-def y_move(array, k):
-    return permute(array, lambda y, z, x, c: (y + k, z, x, c))
 
 
 def adam(grad, weight, first, second):
@@ -451,64 +446,71 @@
     jump = jnp.clip(swap_mask[0] // 2, 0, len(jumps) - 1)
     bits = [swap_mask // 2**bit % 2 for bit in range(SWAP_BITS)]
 
-    where = [lax.axis_index(a) for a in ("y", "zh", "x", "c")]
+    where = [lax.axis_index(a) for a in ("x", "c")]
     where = jnp.stack(where).astype(jnp.int32)
 
     dest = jnp.arange(8, dtype=jnp.int32)
-    ring = (where[2] + dest // 2) % N_X * 2 + (where[3] + dest) % 2
+    ring = (where[0] + dest // 2) % N_X * 2 + (where[1] + dest) % 2
     dest = jnp.concatenate([dest, ring])
     held_at = (dest // 2) * 8 + lax.axis_index("zl") * 2 + dest % 2
     ids = jnp.arange(experts, dtype=jnp.int32)
     here = jnp.sum(jnp.where(placement[None, :] == held_at[:, None], ids[None, :], 0), axis=1)
     here = jnp.broadcast_to(here.astype(jnp.float32)[:, None], (16, tok_rows))
-    pad = jnp.zeros((8 - top, tok_rows), jnp.float32)
-    meta = jnp.concatenate([expert_ids.T.astype(jnp.float32), pad, route_weight.T, pad], axis=0)
-
-    plan = make_plan(cap, top, here, z_gather(meta))
-    x_parts = z_gather(tokens)
+    numbers = jnp.pad(expert_ids.astype(jnp.float32), ((0, 0), (0, 128 - top)))
+    meta = numbers + jnp.pad(route_weight, ((0, 0), (8, 120 - top)))
+
+    x_parts = z_gather(mark(tokens, meta))
+    plan = make_plan(cap, top, here, x_parts)
     state = hold((down_weight[0], first_moment[0], second_moment[0]))
     far_state = swap(state, x=1)
-    x_send = select_rows(False, cap, plan, x_parts, far_state)
+    x_send = select_rows(False, cap, plan, x_parts, 0, width, far_state)
     x_rows = plane_exchange(x_send)
-    g_parts = z_gather(hold((out_grad,), x_send))
+    g_parts = z_gather(hold((out_grad,), x_parts[3]))
     state = choose(bits[3], far_state, state, x_send)
     state_cores = choose(bits[0], swap(state, c=1), state, g_parts[1], g_parts[2])
     state = choose(bits[1], swap(state_cores, zl=1), state_cores)
     state_far = swap(state, zl=2)
 
-    g_send = select_rows(True, cap, plan, g_parts, x_rows, state_cores)
-    g_rows = plane_permute(g_send)
+    chunk = width // G_CHUNKS
+    g_sends = []
+    for i in range(G_CHUNKS):
+        earlier = [x_rows, state_cores] + [g[3] for g in g_sends]
+        g_sends.append(select_rows(True, cap, plan, g_parts, i * chunk, chunk, *earlier))
+    g_rows = [plane_permute(g) for g in g_sends]
 
     down_full = lax.all_gather(down_weight[0], ("y", "zh"), axis=0, tiled=True)
 
-    hidden, turned = hidden_rows(where, [x_rows], gate_weight[0], up_weight[0], g_send[3])
+    hidden = hidden_rows([x_rows], gate_weight[0], up_weight[0], [g[3] for g in g_sends] + [state])
 
     chunk = width // R_CHUNKS
-    r_sends = [down_rows(hidden, down_full, cap, i * chunk, chunk) for i in range(R_CHUNKS)]
+    r_sends = []
+    for i in range(R_CHUNKS):
+        earlier = g_rows[i % G_CHUNKS][1:] if i else ()
+        r_sends.append(down_rows(hidden, down_full, cap, i * chunk, chunk, *earlier))
     returned = [plane_exchange(r) for r in r_sends]
 
-    g_rows = (*g_rows, core_permute(g_rows, r_sends[0], state))
-    state = jnp.split(choose(bits[2], state_far, state, r_sends[0]), 3, axis=0)
-
-    halves = []
-    chunk = width // G_CHUNKS
-    for i in range(G_CHUNKS):
-        blocks = grad_blocks(where, turned, g_rows, i * chunk, chunk)
-        blocks = [blocks[0]] + [y_move(blocks[k], k) for k in (1, 2, 3)]
-        halves.append(sum_blocks(blocks, returned[0]))
-    total = jnp.concatenate(halves, axis=1)
-    total = jnp.where(bits[0][0] == 1, swap(total, c=1), total)
-    rows = total.shape[0] // 2
-    mine, theirs = lax.switch(
-        jump,
-        [lambda a, b, m=m: (relocate(a, m), relocate(b, m, True)) for m in jumps],
-        total[:rows],
-        total[rows:],
-    )
-    grad = mine.astype(jnp.float32) + theirs.astype(jnp.float32)
-    new_state = adam(grad, *state)
-
-    layer_out = jnp.concatenate([z_return(*combine_rows(plan, r)) for r in returned], axis=1)
+    near_state = state
+    state = choose(bits[2], state_far, state, r_sends[0])
+
+    grads, partial, zh = [], None, lax.axis_index("zh")
+    for i, g in enumerate(g_rows):
+        earlier = (near_state,) if partial is None else (partial, *returned[:i])
+        passed = core_permute(g, r_sends[i % R_CHUNKS], *earlier)
+        partial = grad_partial(where, hidden, (*g, passed))
+        total = lax.psum_scatter(partial, "y", scatter_dimension=0, tiled=True)
+        total = choose(bits[0], swap(total, c=1), total, *returned[1 : i + 1])
+        rows = total.shape[0] // 2
+        mine, theirs = lax.switch(
+            jump,
+            [lambda a, b, m=m: (relocate(a, m), relocate(b, m, True)) for m in jumps],
+            lax.dynamic_slice_in_dim(total, zh * rows, rows),
+            lax.dynamic_slice_in_dim(total, (1 - zh) * rows, rows),
+        )
+        grads.append(mine.astype(jnp.float32) + theirs.astype(jnp.float32))
+    new_state = adam(jnp.concatenate(grads, axis=1), *jnp.split(state, 3, axis=0))
+
+    sums = [combine_rows(plan, r, *grads[:i]) for i, r in enumerate(returned)]
+    layer_out = jnp.concatenate([z_return(*s) for s in sums], axis=1)
     return (layer_out, *new_state)
 
 

time: 325 us -> 471 us (1.45); the launches traced: 323 us -> 462 us
  waiting for transfers between devices: 158 us -> 258 us
  Pallas kernels: 78.3 us -> 99.1 us
  local copies, waits for them, and re-layouts: 6.73 us -> 18.8 us
  starting transfers between devices: 57.9 us -> 63 us
    ppermute x26 -> x30, waiting for transfers between devices: 142 us -> 257 us  [permute(): return lax.ppermute(array, AXES, pairs)]
    all_to_all x2 -> x3, waiting for transfers between devices: 15.9 us -> 0.01 us  [plane_exchange(): lax.all_to_all(rows, ('x', 'c'), split_axis=0, concat_axis=0, tiled=True)]
    unnamed x43 -> x63, local copies, waits for them, and re-layouts: 6.59 us -> 15.7 us
    ppermute x26 -> x30, starting transfers between devices: 40.9 us -> 47.7 us  [permute(): return lax.ppermute(array, AXES, pairs)]
    pallas_call x1 -> x2, Pallas kernels: 8.21 us -> 12.5 us  [down_rows(): pl.pallas_call(down_kernel, grid=(width // tile,), in_specs=[pl.BlockSpec...]
    pallas_call x1 -> x2, Pallas kernels: 8.99 us -> 13.2 us  [combine_rows(): pl.pallas_call(combine_kernel, grid=(width // tile,), in_specs=[whole, wh...]
    pallas_call x4 -> x6, Pallas kernels: 12.5 us -> 16.4 us  [choose(): pl.pallas_call(choose_kernel, in_specs=[pl.BlockSpec(memory_space=pltpu.S...]
    pallas_call x2 -> x3, Pallas kernels: 13.8 us -> 17.6 us  [select_rows(): pl.pallas_call(lambda *refs: select_kernel(scaled, *refs), grid=(width //...]
  transfers between devices with their start and end apart: 29 -> 36, of which waited for: 14 -> 17; matrix products, arithmetic and copies ran while one was open for 2% -> 2% of each run, Pallas kernels for 24% -> 19%
where the time goes in v1:
time: 471 us; the launch traced here: 462 us
  waiting for transfers between devices  258 us (55%)
  Pallas kernels  99.1 us (21%)
  starting transfers between devices  63 us (13%)
  local copies, waits for them, and re-layouts  18.8 us (4%)
  between operations  15.1 us (3%)
  other arithmetic  8.33 us (2%)
    ppermute x30, waiting for transfers between devices, permute(): return lax.ppermute(array, AXES, pairs)  257 us
    ppermute x30, starting transfers between devices, permute(): return lax.ppermute(array, AXES, pairs)  47.7 us
    pallas_call x3, Pallas kernels, select_rows(): pl.pallas_call(lambda *refs: select_kernel(scaled, *refs), grid=(width //...  17.6 us
    pallas_call x6, Pallas kernels, choose(): pl.pallas_call(choose_kernel, in_specs=[pl.BlockSpec(memory_space=pltpu.S...  16.4 us
    unnamed x63, local copies, waits for them, and re-layouts  15.7 us
    all_to_all x3, starting transfers between devices, plane_exchange(): lax.all_to_all(rows, ('x', 'c'), split_axis=0, concat_axis=0, tiled=True)  15.2 us
    pallas_call x2, Pallas kernels, grad_partial(): pl.pallas_call(grad_kernel, grid=(width // tile,), in_specs=[pl.BlockSpec...  14.1 us
    pallas_call x2, Pallas kernels, combine_rows(): pl.pallas_call(combine_kernel, grid=(width // tile,), in_specs=[whole, wh...  13.2 us
  transfers between devices with their start and end apart: 36, of which 17 were waited for; matrix products, arithmetic and copies ran while one was open for 2% of the time, Pallas kernels for 19%

profile of v1, /device:TPU:1, one launch (start us, length us, event | category | flops | bytes accessed | tf_op | source)
XLA Modules:
  0.0 462.4 jit_solution(862283230652367246)
XLA Ops:
  7.9 2.6 hold.4.own
  10.5 2.0 collective-permute-start.33
  13.5 2.0 mark.1.refs_1_.refs_2_
  15.5 5.6 %collective-permute-start.30 = (bf16[128,2688]{1,0:T(8,128)(2,1)}, bf16[128,2688]{1,0:T(8,128)(2,1)S(1)}, u32[]{:S(2)}, u32[]{:S(2)}) collective-permute-start(bf16[128,2688]{1,0:T(8,128)(2,1)} %mark.1.refs_1_.refs_2_), channel_id=1, source_target_pairs={{0,2},{1,39},{8,10},{9,47},{16,18},{17,55},{24,26},{25,63},{2,4},{... | collective-permute-start | bytes 2064392 | tf_op jit(solution)/shard_map/ppermute | solution.py:34
  21.1 24.3 %collective-permute-done.30.refs_2_.refs_3_ = bf16[128,2688]{1,0:T(8,128)(2,1)S(1)} collective-permute-done((bf16[128,2688]{1,0:T(8,128)(2,1)}, bf16[128,2688]{1,0:T(8,128)(2,1)S(1)}, u32[]{:S(2)}, u32[]{:S(2)}) %collective-permute-start.30) | collective-permute-done | bytes 688160 | tf_op jit(solution)/shard_map/ppermute | solution.py:34
  45.4 3.7 collective-permute-start.32
  49.4 7.6 %collective-permute-done.32.refs_4_.refs_5_.refs_1_ = bf16[128,2688]{1,0:T(8,128)(2,1)S(1)} collective-permute-done((bf16[128,2688]{1,0:T(8,128)(2,1)S(1)}, bf16[128,2688]{1,0:T(8,128)(2,1)S(1)}, u32[]{:S(2)}, u32[]{:S(2)}) %collective-permute-start.32) | collective-permute-done | bytes 688160 | tf_op jit(solution)/shard_map/ppermute | solution.py:34
  57.8 1.7 plan.1
  60.6 7.1 %select.94.refs_0_ = bf16[8,112,2560]{2,1,0:T(8,128)(2,1)} custom-call(f32[16,512]{1,0:T(8,128)} %get-tuple-element.138.refs_0_.slots, f32[16,512]{1,0:T(8,128)} %get-tuple-element.139.refs_1_.weights, bf16[128,2688]{1,0:T(8,128)(2,1)} %mark.1.refs_1_.refs_2_, bf16[128,2688]{1,0:T(8,128)(2,1)} %copy-done.11, bf16[128,2688]{1,0:T(8,128)(2,1)} %copy-done.12, ...), custom_call_target="tpu_custom_call" | custom-call | flops 1 | bytes 1 | tf_op jit(solution)/shard_map/select/pallas_call | solution.py:231
  67.7 6.7 %all-to-all-start = ((bf16[8,112,2560]{2,1,0:T(8,128)(2,1)}), bf16[8,112,2560]{2,1,0:T(8,128)(2,1)}, u32[]{:S(2)}, u32[]{:S(2)}) async-start(bf16[8,112,2560]{2,1,0:T(8,128)(2,1)} %select.94.refs_0_), calls=%async_computation | async-start | bytes 9175040 | tf_op jit(solution)/shard_map/all_to_all | solution.py:409
  75.1 3.0 choose.6.own
  78.3 2.0 hold.5.refs_2_
  80.3 1.5 collective-permute-start.34
  81.8 39.0 %collective-permute-done.34.refs_0_.refs_3_ = bf16[128,2560]{1,0:T(8,128)(2,1)S(1)} collective-permute-done((bf16[128,2560]{1,0:T(8,128)(2,1)}, bf16[128,2560]{1,0:T(8,128)(2,1)S(1)}, u32[]{:S(2)}, u32[]{:S(2)}) %collective-permute-start.34) | collective-permute-done | bytes 655392 | tf_op jit(solution)/shard_map/ppermute | solution.py:34
  120.8 2.6 collective-permute-done.35.refs_1_.refs_4_
  125.3 3.1 choose.7.refs_7_.own
  128.4 2.3 collective-permute-start.36
  130.7 38.9 %collective-permute-done.36.refs_5_ = bf16[128,2560]{1,0:T(8,128)(2,1)S(1)} collective-permute-done((bf16[128,2560]{1,0:T(8,128)(2,1)}, bf16[128,2560]{1,0:T(8,128)(2,1)S(1)}, u32[]{:S(2)}, u32[]{:S(2)}) %collective-permute-start.36) | collective-permute-done | bytes 655392 | tf_op jit(solution)/shard_map/ppermute | solution.py:34
  170.5 5.2 %select_scaled.2 = (bf16[224,1280]{1,0:T(8,128)(2,1)}, bf16[224,1280]{1,0:T(8,128)(2,1)}, bf16[224,1280]{1,0:T(8,128)(2,1)}, bf16[224,1280]{1,0:T(8,128)(2,1)}) custom-call(f32[16,512]{1,0:T(8,128)} %get-tuple-element.138.refs_0_.slots, f32[16,512]{1,0:T(8,128)} %get-tuple-element.139.refs_1_.weights, bf16[128,2560]{1,0:T(8,128)(2,1)} %hold.5.refs_2_, ...), custom_call_target="tpu_custom_call" | custom-call | flops 1 | bytes 1 | tf_op jit(solution)/shard_map/select_scaled/pallas_call | solution.py:231
  176.8 2.6 collective-permute-start.46
  181.5 3.2 choose.8.refs_5_.own
  184.7 5.2 %select_scaled.3 = (bf16[224,1280]{1,0:T(8,128)(2,1)}, bf16[224,1280]{1,0:T(8,128)(2,1)}, bf16[224,1280]{1,0:T(8,128)(2,1)}, bf16[224,1280]{1,0:T(8,128)(2,1)}) custom-call(f32[16,512]{1,0:T(8,128)} %get-tuple-element.138.refs_0_.slots, f32[16,512]{1,0:T(8,128)} %get-tuple-element.139.refs_1_.weights, bf16[128,2560]{1,0:T(8,128)(2,1)} %hold.5.refs_2_, ...), custom_call_target="tpu_custom_call" | custom-call | flops 1 | bytes 1 | tf_op jit(solution)/shard_map/select_scaled/pallas_call | solution.py:231
  190.0 11.7 %hidden.1 = bf16[896,768]{1,0:T(8,128)(2,1)} custom-call(bf16[8,112,2560]{2,1,0:T(8,128)(2,1)} %all-to-all-done.refs_6_.refs_0_, bf16[2560,768]{1,0:T(8,128)(2,1)} %bitcast.21, bf16[2560,768]{1,0:T(8,128)(2,1)} %bitcast.22, bf16[224,1280]{1,0:T(8,128)(2,1)} %get-tuple-element.140.refs_8_.refs_3_, bf16[224,1280]{1,0:T(8,128)(2,1)} %get-tuple-element.141.refs_4_, ...), custom_call_target="tpu_custom_call" | custom-call | flops 1 | bytes 1 | tf_op jit(solution)/shard_map/hidden/pallas_call | solution.py:266
  201.7 6.3 %down.2.refs_4_.refs_0_ = bf16[8,112,1280]{2,1,0:T(8,128)(2,1)} custom-call(bf16[896,768]{1,0:T(8,128)(2,1)} %hidden.1, bf16[768,2560]{1,0:T(8,128)(2,1)} %bitcast.19), custom_call_target="tpu_custom_call" | custom-call | flops 1 | bytes 1 | tf_op jit(solution)/shard_map/down/pallas_call | solution.py:290
  209.2 2.7 hold.6
  212.5 2.4 collective-permute-done.48.refs_4_
  215.9 7.1 %grad.2.refs_5_ = bf16[768,1280]{1,0:T(8,128)(2,1)} custom-call(s32[2]{0:T(128)} %pad_add_fusion.2.where, bf16[896,768]{1,0:T(8,128)(2,1)} %hidden.1, bf16[224,1280]{1,0:T(8,128)(2,1)} %get-tuple-element.148.refs_0_, bf16[224,1280]{1,0:T(8,128)(2,1)} %copy-done.14, bf16[224,1280]{1,0:T(8,128)(2,1)} %copy-done.15, bf16[224,1280]{1,0:T(8,128)(2,1)} %copy-done.16, ...), custom_call_target="tpu_custom_call" | custom-call | flops 1 | bytes 1 | tf_op jit(solution)/shard_map/grad/pallas_call | solution.py:326
  223.0 3.7 all-to-all-start.1
  226.7 1.4 collective-permute-start.42
  228.1 2.4 collective-permute-start.43
  230.5 1.2 collective-permute-start.44
  231.6 35.6 %collective-permute-done.42.refs_0_.refs_1_ = bf16[224,1280]{1,0:T(8,128)(2,1)S(1)} collective-permute-done((bf16[224,1280]{1,0:T(8,128)(2,1)}, bf16[224,1280]{1,0:T(8,128)(2,1)S(1)}, u32[]{:S(2)}, u32[]{:S(2)}) %collective-permute-start.42) | collective-permute-done | bytes 573472 | tf_op jit(solution)/shard_map/ppermute | solution.py:34
  267.3 12.4 %collective-permute-done.43.refs_1_.refs_2_ = bf16[224,1280]{1,0:T(8,128)(2,1)S(1)} collective-permute-done((bf16[224,1280]{1,0:T(8,128)(2,1)}, bf16[224,1280]{1,0:T(8,128)(2,1)S(1)}, u32[]{:S(2)}, u32[]{:S(2)}) %collective-permute-start.43) | collective-permute-done | bytes 573472 | tf_op jit(solution)/shard_map/ppermute | solution.py:34
  281.4 6.2 %down.3.refs_4_ = bf16[8,112,1280]{2,1,0:T(8,128)(2,1)} custom-call(bf16[896,768]{1,0:T(8,128)(2,1)} %hidden.1, bf16[768,2560]{1,0:T(8,128)(2,1)} %bitcast.20, bf16[224,1280]{1,0:T(8,128)(2,1)} %copy-done.7, bf16[224,1280]{1,0:T(8,128)(2,1)} %copy-done.8, bf16[224,1280]{1,0:T(8,128)(2,1)} %copy-done.9), custom_call_target="tpu_custom_call" | custom-call | flops 1 | bytes 1 | tf_op jit(solution)/shard_map/down/pallas_call | solution.py:290
  287.6 1.5 copy-done.1
  289.1 2.7 hold.7
  292.6 2.6 collective-permute-done.54.refs_4_
  296.3 7.1 %grad.3 = bf16[768,1280]{1,0:T(8,128)(2,1)} custom-call(s32[2]{0:T(128)} %pad_add_fusion.2.where, bf16[896,768]{1,0:T(8,128)(2,1)} %hidden.1, bf16[224,1280]{1,0:T(8,128)(2,1)} %get-tuple-element.157.refs_0_, bf16[224,1280]{1,0:T(8,128)(2,1)} %copy-done.7, bf16[224,1280]{1,0:T(8,128)(2,1)} %copy-done.8, bf16[224,1280]{1,0:T(8,128)(2,1)} %copy-done.9, ...), custom_call_target="tpu_custom_call" | custom-call | flops 1 | bytes 1 | tf_op jit(solution)/shard_map/grad/pallas_call | solution.py:326
  303.4 1.3 copy-done
  305.8 4.9 %all-to-all-start.2 = ((bf16[8,112,1280]{2,1,0:T(8,128)(2,1)}), bf16[8,112,1280]{2,1,0:T(8,128)(2,1)}, u32[]{:S(2)}, u32[]{:S(2)}) async-start(bf16[8,112,1280]{2,1,0:T(8,128)(2,1)} %down.3.refs_4_), calls=%async_computation.2 | async-start | bytes 4587520 | tf_op jit(solution)/shard_map/all_to_all | solution.py:409
  310.9 59.9 %collective-permute-done.53.other = bf16[288,2560]{1,0:T(8,128)(2,1)S(1)} collective-permute-done((bf16[288,2560]{1,0:T(8,128)(2,1)S(1)}, bf16[288,2560]{1,0:T(8,128)(2,1)S(1)}, u32[]{:S(2)}, u32[]{:S(2)}) %collective-permute-start.53) | collective-permute-done | bytes 1474592 | tf_op jit(solution)/shard_map/ppermute | solution.py:34
  371.9 3.0 choose.10
  374.9 6.6 %combine.2 = (f32[128,1280]{1,0:T(8,128)}, bf16[128,1280]{1,0:T(8,128)(2,1)}, bf16[128,1280]{1,0:T(8,128)(2,1)}, bf16[128,1280]{1,0:T(8,128)(2,1)}) custom-call(f32[16,512]{1,0:T(8,128)} %get-tuple-element.138.refs_0_.slots, f32[16,512]{1,0:T(8,128)} %get-tuple-element.139.refs_1_.weights, bf16[8,112,1280]{2,1,0:T(8,128)(2,1)} %copy-done.1), custom_call_target="tpu_custom_call" | custom-call | flops 1 | bytes 1 | tf_op jit(solution)/shard_map/combine/pallas_call | solution.py:376
  381.6 3.2 collective-permute-start.41
  385.6 2.0 choose.9
  388.6 13.8 %conditional.8 = (bf16[96,1280]{1,0:T(8,128)(2,1)S(1)}, bf16[96,1280]{1,0:T(8,128)(2,1)}) conditional(s32[]{:T(128)} %clamp.4, (bf16[96,1280]{1,0:T(8,128)(2,1)S(1)}, bf16[96,1280]{1,0:T(8,128)(2,1)S(1)}) %tuple.140, (bf16[96,1280]{1,0:T(8,128)(2,1)S(1)}, ...), branch_computations={%region_2.3_spmd, %region_3.4_spmd, %region_4.5_spmd, %region_5.6_... | conditional | bytes 2457696
  388.8 2.6 collective-permute-start.2
  391.4 10.2 %collective-permute-done.1 = bf16[96,1280]{1,0:T(8,128)(2,1)S(1)} collective-permute-done((bf16[96,1280]{1,0:T(8,128)(2,1)S(1)}, bf16[96,1280]{1,0:T(8,128)(2,1)S(1)}, u32[]{:S(2)}, u32[]{:S(2)}) %collective-permute-start.1) | collective-permute-done | bytes 245792 | tf_op jit(solution)/shard_map/cond/branch_1_fun/ppermute | solution.py:34
  402.5 1.8 convert_add_fusion.1.refs_0_
  404.2 6.6 %combine.3 = (f32[128,1280]{1,0:T(8,128)}, bf16[128,1280]{1,0:T(8,128)(2,1)}, bf16[128,1280]{1,0:T(8,128)(2,1)}, bf16[128,1280]{1,0:T(8,128)(2,1)}) custom-call(f32[16,512]{1,0:T(8,128)} %get-tuple-element.138.refs_0_.slots, f32[16,512]{1,0:T(8,128)} %get-tuple-element.139.refs_1_.weights, bf16[8,112,1280]{2,1,0:T(8,128)(2,1)} %all-to-all-done.2.rows.refs_0_, ...), custom_call_target="tpu_custom_call" | custom-call | flops 1 | bytes 1 | tf_op jit(solution)/shard_map/combine/pallas_call | solution.py:376
  410.9 4.1 collective-permute-start.50
  415.1 2.9 collective-permute-start.52
  418.0 1.7 collective-permute-done.50
  420.8 2.2 collective-permute-start.51
  422.9 3.3 collective-permute-done.40
  426.3 1.8 collective-permute-start.55
  428.2 1.5 collective-permute-done.51
  431.5 2.0 choose.11
  434.6 18.1 %conditional.9 = (bf16[96,1280]{1,0:T(8,128)(2,1)S(1)}, bf16[96,1280]{1,0:T(8,128)(2,1)}) conditional(s32[]{:T(128)} %clamp.4, (bf16[96,1280]{1,0:T(8,128)(2,1)S(1)}, bf16[96,1280]{1,0:T(8,128)(2,1)S(1)}) %tuple.142, (bf16[96,1280]{1,0:T(8,128)(2,1)S(1)}, ...), branch_computations={%region_11.12_spmd, %region_12.13_spmd, %region_13.14_spmd, %regio... | conditional | bytes 2457696
  434.6 2.3 collective-permute-start.16
  436.9 1.4 collective-permute-start.17
  438.3 7.0 %collective-permute-done.16 = bf16[96,1280]{1,0:T(8,128)(2,1)S(1)} collective-permute-done((bf16[96,1280]{1,0:T(8,128)(2,1)S(1)}, bf16[96,1280]{1,0:T(8,128)(2,1)S(1)}, u32[]{:S(2)}, u32[]{:S(2)}) %collective-permute-start.16) | collective-permute-done | bytes 245792 | tf_op jit(solution)/shard_map/cond/branch_1_fun/ppermute | solution.py:34
  445.3 7.4 %collective-permute-done.17 = bf16[96,1280]{1,0:T(8,128)(2,1)} collective-permute-done((bf16[96,1280]{1,0:T(8,128)(2,1)S(1)}, bf16[96,1280]{1,0:T(8,128)(2,1)}, u32[]{:S(2)}, u32[]{:S(2)}) %collective-permute-start.17) | collective-permute-done | bytes 245792 | tf_op jit(solution)/shard_map/cond/branch_1_fun/ppermute | solution.py:34
  453.7 1.7 convert_bitcast_fusion
  (118 shorter events, 27.2 us)
Async XLA Ops:
  7.2 194.6 %all-gather.3.cloned.1.call-start = ((), (), s32[]{:S(2)}) async-start(), calls=%async_computation.7 | async-start | bytes 4423680 | tf_op jit(solution)/shard_map/all_gather | solution.py:481
  7.9 4.6 %copy-start.28 = (s32[128,6]{0,1:T(8,128)S(1)}, s32[128,6]{0,1:T(8,128)}, u32[]{:S(2)}) copy-start(s32[128,6]{0,1:T(8,128)} %param.28) | copy-start | bytes 9220
  7.9 4.7 %copy-start.27 = (f32[128,6]{0,1:T(8,128)S(1)}, f32[128,6]{0,1:T(8,128)}, u32[]{:S(2)}) copy-start(f32[128,6]{0,1:T(8,128)} %param.29) | copy-start | bytes 9220
  10.5 38.7 %copy-start.29 = (s32[32]{0:T(128)S(1)}, s32[32]{0:T(128)}, u32[]{:S(2)}) copy-start(s32[32]{0:T(128)} %param.30) | copy-start | bytes 388
  10.5 49.0 %collective-permute-start.33 = (bf16[288,2560]{1,0:T(8,128)(2,1)}, bf16[288,2560]{1,0:T(8,128)(2,1)S(1)}, u32[]{:S(2)}, u32[]{:S(2)}) collective-permute-start(bf16[288,2560]{1,0:T(8,128)(2,1)} %hold.4.own), channel_id=1, source_target_pairs={{0,8},{1,9},{8,0},{9,1},{16,24},{17,25},{24,16},{25,17},{2,10},{3,... | collective-permute-start | bytes 4423688 | tf_op jit(solution)/shard_map/ppermute | solution.py:34
  15.5 29.9 %collective-permute-start.30 = (bf16[128,2688]{1,0:T(8,128)(2,1)}, bf16[128,2688]{1,0:T(8,128)(2,1)S(1)}, u32[]{:S(2)}, u32[]{:S(2)}) collective-permute-start(bf16[128,2688]{1,0:T(8,128)(2,1)} %mark.1.refs_1_.refs_2_), channel_id=1, source_target_pairs={{0,2},{1,39},{8,10},{9,47},{16,18},{17,55},{24,26},{25,63},{2,4},{... | collective-permute-start | bytes 2064392 | tf_op jit(solution)/shard_map/ppermute | solution.py:34
  21.1 28.3 %collective-permute-start.31 = (bf16[128,2688]{1,0:T(8,128)(2,1)}, bf16[128,2688]{1,0:T(8,128)(2,1)S(1)}, u32[]{:S(2)}, u32[]{:S(2)}) collective-permute-start(bf16[128,2688]{1,0:T(8,128)(2,1)} %mark.1.refs_1_.refs_2_), channel_id=1, source_target_pairs={{0,38},{1,3},{8,46},{9,11},{16,54},{17,19},{24,62},{25,27},{2,0},{... | collective-permute-start | bytes 2064392 | tf_op jit(solution)/shard_map/ppermute | solution.py:34
  45.4 12.3 %copy-start.11 = (bf16[128,2688]{1,0:T(8,128)(2,1)}, bf16[128,2688]{1,0:T(8,128)(2,1)S(1)}, u32[]{:S(2)}) copy-start(bf16[128,2688]{1,0:T(8,128)(2,1)S(1)} %collective-permute-done.30.refs_2_.refs_3_) | copy-start | bytes 2064388
  45.4 11.6 %collective-permute-start.32 = (bf16[128,2688]{1,0:T(8,128)(2,1)S(1)}, bf16[128,2688]{1,0:T(8,128)(2,1)S(1)}, u32[]{:S(2)}, u32[]{:S(2)}) collective-permute-start(bf16[128,2688]{1,0:T(8,128)(2,1)S(1)} %collective-permute-done.30.refs_2_.refs_3_), channel_id=1, source_target_pairs={{0,2},{1,39},{8,10},{9,47},{16,18},{17,55},{24,26},{25,63},{2,4},{... | collective-permute-start | bytes 2064392 | tf_op jit(solution)/shard_map/ppermute | solution.py:34
  49.4 8.3 %copy-start.12 = (bf16[128,2688]{1,0:T(8,128)(2,1)}, bf16[128,2688]{1,0:T(8,128)(2,1)S(1)}, u32[]{:S(2)}) copy-start(bf16[128,2688]{1,0:T(8,128)(2,1)S(1)} %collective-permute-done.31.refs_3_.refs_4_) | copy-start | bytes 2064388
  57.0 0.9 copy-start.2
  59.5 1.1 copy-start.5
  67.7 101.9 %all-to-all-start = ((bf16[8,112,2560]{2,1,0:T(8,128)(2,1)}), bf16[8,112,2560]{2,1,0:T(8,128)(2,1)}, u32[]{:S(2)}, u32[]{:S(2)}) async-start(bf16[8,112,2560]{2,1,0:T(8,128)(2,1)} %select.94.refs_0_), calls=%async_computation | async-start | bytes 9175040 | tf_op jit(solution)/shard_map/all_to_all | solution.py:409
  74.4 236.2 %reduce-scatter.3.cloned.1.call-start = ((), (), s32[]{:S(2)}) async-start(), calls=%async_computation.5 | async-start | bytes 2457600 | tf_op jit(solution)/shard_map/reduce_scatter | solution.py:500
  78.1 45.3 %collective-permute-start.37 = (bf16[288,2560]{1,0:T(8,128)(2,1)}, bf16[288,2560]{1,0:T(8,128)(2,1)S(1)}, u32[]{:S(2)}, u32[]{:S(2)}) collective-permute-start(bf16[288,2560]{1,0:T(8,128)(2,1)} %choose.6.own), channel_id=1, source_target_pairs={{0,1},{1,0},{8,9},{9,8},{16,17},{17,16},{24,25},{25,24},{2,3},{3,2... | collective-permute-start | bytes 4423688 | tf_op jit(solution)/shard_map/ppermute | solution.py:34
  80.3 40.5 %collective-permute-start.34 = (bf16[128,2560]{1,0:T(8,128)(2,1)}, bf16[128,2560]{1,0:T(8,128)(2,1)S(1)}, u32[]{:S(2)}, u32[]{:S(2)}) collective-permute-start(bf16[128,2560]{1,0:T(8,128)(2,1)} %hold.5.refs_2_), channel_id=1, source_target_pairs={{0,2},{1,39},{8,10},{9,47},{16,18},{17,55},{24,26},{25,63},{2,4},{... | collective-permute-start | bytes 1966088 | tf_op jit(solution)/shard_map/ppermute | solution.py:34
  81.8 41.6 %collective-permute-start.35 = (bf16[128,2560]{1,0:T(8,128)(2,1)}, bf16[128,2560]{1,0:T(8,128)(2,1)S(1)}, u32[]{:S(2)}, u32[]{:S(2)}) collective-permute-start(bf16[128,2560]{1,0:T(8,128)(2,1)} %hold.5.refs_2_), channel_id=1, source_target_pairs={{0,38},{1,3},{8,46},{9,11},{16,54},{17,19},{24,62},{25,27},{2,0},{... | collective-permute-start | bytes 1966088 | tf_op jit(solution)/shard_map/ppermute | solution.py:34
  120.8 2.6 copy-start.3
  123.4 0.8 copy-start.4
  124.2 1.1 copy-start.19
  128.4 52.0 %collective-permute-start.38 = (bf16[288,2560]{1,0:T(8,128)(2,1)}, bf16[288,2560]{1,0:T(8,128)(2,1)S(1)}, u32[]{:S(2)}, u32[]{:S(2)}) collective-permute-start(bf16[288,2560]{1,0:T(8,128)(2,1)} %choose.7.refs_7_.own), channel_id=1, source_target_pairs={{0,2},{1,3},{8,10},{9,11},{16,18},{17,19},{24,26},{25,27},{2,0},{3... | collective-permute-start | bytes 4423688 | tf_op jit(solution)/shard_map/ppermute | solution.py:34
  128.4 41.2 %collective-permute-start.36 = (bf16[128,2560]{1,0:T(8,128)(2,1)}, bf16[128,2560]{1,0:T(8,128)(2,1)S(1)}, u32[]{:S(2)}, u32[]{:S(2)}) collective-permute-start(bf16[128,2560]{1,0:T(8,128)(2,1)} %copy-done.3), channel_id=1, source_target_pairs={{0,2},{1,39},{8,10},{9,47},{16,18},{17,55},{24,26},{25,63},{2,4},{... | collective-permute-start | bytes 1966088 | tf_op jit(solution)/shard_map/ppermute | solution.py:34
  169.6 0.9 copy-start.13
  175.7 32.2 %collective-permute-start.45 = (bf16[224,1280]{1,0:T(8,128)(2,1)}, bf16[224,1280]{1,0:T(8,128)(2,1)S(1)}, u32[]{:S(2)}, u32[]{:S(2)}) collective-permute-start(bf16[224,1280]{1,0:T(8,128)(2,1)} %get-tuple-element.149), channel_id=1, source_target_pairs={{0,8},{1,9},{8,16},{9,17},{16,24},{17,25},{24,0},{25,1},{2,10},{3,... | collective-permute-start | bytes 1720328 | tf_op jit(solution)/shard_map/ppermute | solution.py:34
  176.8 31.2 %collective-permute-start.46 = (bf16[224,1280]{1,0:T(8,128)(2,1)}, bf16[224,1280]{1,0:T(8,128)(2,1)S(1)}, u32[]{:S(2)}, u32[]{:S(2)}) collective-permute-start(bf16[224,1280]{1,0:T(8,128)(2,1)} %get-tuple-element.150), channel_id=1, source_target_pairs={{0,16},{1,17},{8,24},{9,25},{16,0},{17,1},{24,8},{25,9},{2,18},{3,... | collective-permute-start | bytes 1720328 | tf_op jit(solution)/shard_map/ppermute | solution.py:34
  179.4 28.6 %collective-permute-start.47 = (bf16[224,1280]{1,0:T(8,128)(2,1)}, bf16[224,1280]{1,0:T(8,128)(2,1)S(1)}, u32[]{:S(2)}, u32[]{:S(2)}) collective-permute-start(bf16[224,1280]{1,0:T(8,128)(2,1)} %get-tuple-element.140.refs_8_.refs_3_), channel_id=1, source_target_pairs={{0,24},{1,25},{8,0},{9,1},{16,8},{17,9},{24,16},{25,17},{2,26},{3,... | collective-permute-start | bytes 1720328 | tf_op jit(solution)/shard_map/ppermute | solution.py:34
  180.4 1.1 copy-start.18
  208.0 0.8 copy-start.14
  208.0 1.0 copy-start.15
  208.0 1.2 copy-start.16
  211.8 3.0 collective-permute-start.48
  214.8 1.1 copy-start.20
  223.0 64.6 %all-to-all-start.1 = ((bf16[8,112,1280]{2,1,0:T(8,128)(2,1)}), bf16[8,112,1280]{2,1,0:T(8,128)(2,1)S(1)}, u32[]{:S(2)}, u32[]{:S(2)}) async-start(bf16[8,112,1280]{2,1,0:T(8,128)(2,1)} %down.2.refs_4_.refs_0_), calls=%async_computation.1 | async-start | bytes 4587520 | tf_op jit(solution)/shard_map/all_to_all | solution.py:409
  226.7 199.7 %reduce-scatter.5.cloned.1.call-start = ((), (), s32[]{:S(2)}) async-start(), calls=%async_computation.6 | async-start | bytes 2457600 | tf_op jit(solution)/shard_map/reduce_scatter | solution.py:500
  226.7 40.6 %collective-permute-start.42 = (bf16[224,1280]{1,0:T(8,128)(2,1)}, bf16[224,1280]{1,0:T(8,128)(2,1)S(1)}, u32[]{:S(2)}, u32[]{:S(2)}) collective-permute-start(bf16[224,1280]{1,0:T(8,128)(2,1)} %get-tuple-element.146), channel_id=1, source_target_pairs={{0,8},{1,9},{8,16},{9,17},{16,24},{17,25},{24,0},{25,1},{2,10},{3,... | collective-permute-start | bytes 1720328 | tf_op jit(solution)/shard_map/ppermute | solution.py:34
  228.1 51.7 %collective-permute-start.43 = (bf16[224,1280]{1,0:T(8,128)(2,1)}, bf16[224,1280]{1,0:T(8,128)(2,1)S(1)}, u32[]{:S(2)}, u32[]{:S(2)}) collective-permute-start(bf16[224,1280]{1,0:T(8,128)(2,1)} %get-tuple-element.147), channel_id=1, source_target_pairs={{0,16},{1,17},{8,24},{9,25},{16,0},{17,1},{24,8},{25,9},{2,18},{3,... | collective-permute-start | bytes 1720328 | tf_op jit(solution)/shard_map/ppermute | solution.py:34
  230.5 49.3 %collective-permute-start.44 = (bf16[224,1280]{1,0:T(8,128)(2,1)}, bf16[224,1280]{1,0:T(8,128)(2,1)S(1)}, u32[]{:S(2)}, u32[]{:S(2)}) collective-permute-start(bf16[224,1280]{1,0:T(8,128)(2,1)} %get-tuple-element.141.refs_4_), channel_id=1, source_target_pairs={{0,24},{1,25},{8,0},{9,1},{16,8},{17,9},{24,16},{25,17},{2,26},{3,... | collective-permute-start | bytes 1720328 | tf_op jit(solution)/shard_map/ppermute | solution.py:34
  267.3 12.5 %copy-start.7 = (bf16[224,1280]{1,0:T(8,128)(2,1)}, bf16[224,1280]{1,0:T(8,128)(2,1)S(1)}, u32[]{:S(2)}) copy-start(bf16[224,1280]{1,0:T(8,128)(2,1)S(1)} %collective-permute-done.42.refs_0_.refs_1_) | copy-start | bytes 1720324
  279.7 0.8 copy-start.8
  280.6 0.8 copy-start.9
  287.6 1.5 copy-start.1
  291.8 3.5 collective-permute-start.54
  295.3 1.1 copy-start.21
  303.4 1.4 copy-start
  304.8 66.0 %collective-permute-start.53 = (bf16[288,2560]{1,0:T(8,128)(2,1)S(1)}, bf16[288,2560]{1,0:T(8,128)(2,1)S(1)}, u32[]{:S(2)}, u32[]{:S(2)}) collective-permute-start(bf16[288,2560]{1,0:T(8,128)(2,1)S(1)} %copy-done), channel_id=1, source_target_pairs={{0,4},{1,5},{8,12},{9,13},{16,20},{17,21},{24,28},{25,29},{2,6},{3... | collective-permute-start | bytes 4423688 | tf_op jit(solution)/shard_map/ppermute | solution.py:34
  305.8 98.5 %all-to-all-start.2 = ((bf16[8,112,1280]{2,1,0:T(8,128)(2,1)}), bf16[8,112,1280]{2,1,0:T(8,128)(2,1)}, u32[]{:S(2)}, u32[]{:S(2)}) async-start(bf16[8,112,1280]{2,1,0:T(8,128)(2,1)} %down.3.refs_4_), calls=%async_computation.2 | async-start | bytes 4587520 | tf_op jit(solution)/shard_map/all_to_all | solution.py:409
  310.6 74.1 %collective-permute-start.49 = (bf16[192,1280]{1,0:T(8,128)(2,1)}, bf16[192,1280]{1,0:T(8,128)(2,1)S(1)}, u32[]{:S(2)}, u32[]{:S(2)}) collective-permute-start(bf16[192,1280]{1,0:T(8,128)(2,1)} %reduce-scatter.3.cloned.1.call-done.own), channel_id=1, source_target_pairs={{0,1},{1,0},{8,9},{9,8},{16,17},{17,16},{24,25},{25,24},{2,3},{3,2... | collective-permute-start | bytes 1474568 | tf_op jit(solution)/shard_map/ppermute | solution.py:34
  370.8 1.1 copy-start.17
  381.5 33.4 %collective-permute-start.39 = (bf16[128,1280]{1,0:T(8,128)(2,1)}, bf16[128,1280]{1,0:T(8,128)(2,1)S(1)}, u32[]{:S(2)}, u32[]{:S(2)}) collective-permute-start(bf16[128,1280]{1,0:T(8,128)(2,1)} %get-tuple-element.143), channel_id=1, source_target_pairs={{0,38},{1,3},{8,46},{9,11},{16,54},{17,19},{24,62},{25,27},{2,0},{... | collective-permute-start | bytes 983048 | tf_op jit(solution)/shard_map/ppermute | solution.py:34
  381.6 41.3 %collective-permute-start.41 = (bf16[128,1280]{1,0:T(8,128)(2,1)}, bf16[128,1280]{1,0:T(8,128)(2,1)S(1)}, u32[]{:S(2)}, u32[]{:S(2)}) collective-permute-start(bf16[128,1280]{1,0:T(8,128)(2,1)} %get-tuple-element.145), channel_id=1, source_target_pairs={{0,2},{1,39},{8,10},{9,47},{16,18},{17,55},{24,26},{25,63},{2,4},{... | collective-permute-start | bytes 983048 | tf_op jit(solution)/shard_map/ppermute | solution.py:34
  388.7 12.9 %collective-permute-start.1 = (bf16[96,1280]{1,0:T(8,128)(2,1)S(1)}, bf16[96,1280]{1,0:T(8,128)(2,1)S(1)}, u32[]{:S(2)}, u32[]{:S(2)}) collective-permute-start(bf16[96,1280]{1,0:T(8,128)(2,1)S(1)} %get-tuple-element.82), channel_id=1, source_target_pairs={{0,2},{1,3},{8,10},{9,11},{16,18},{17,19},{24,26},{25,27},{2,0},{3... | collective-permute-start | bytes 737288 | tf_op jit(solution)/shard_map/cond/branch_1_fun/ppermute | solution.py:34
  388.8 13.7 %collective-permute-start.2 = (bf16[96,1280]{1,0:T(8,128)(2,1)S(1)}, bf16[96,1280]{1,0:T(8,128)(2,1)}, u32[]{:S(2)}, u32[]{:S(2)}) collective-permute-start(bf16[96,1280]{1,0:T(8,128)(2,1)S(1)} %get-tuple-element.83), channel_id=1, source_target_pairs={{0,34},{1,35},{8,42},{9,43},{16,50},{17,51},{24,58},{25,59},{2,32}... | collective-permute-start | bytes 737288 | tf_op jit(solution)/shard_map/cond/branch_1_fun/ppermute | solution.py:34
  404.2 10.7 %copy-start.26 = (bf16[128,1280]{1,0:T(8,128)(2,1)S(1)}, bf16[128,1280]{1,0:T(8,128)(2,1)}, u32[]{:S(2)}) copy-start(bf16[128,1280]{1,0:T(8,128)(2,1)} %get-tuple-element.144) | copy-start | bytes 983044
  410.9 15.3 %copy-start.22 = (f32[128,1280]{1,0:T(8,128)S(1)}, f32[128,1280]{1,0:T(8,128)}, u32[]{:S(2)}) copy-start(f32[128,1280]{1,0:T(8,128)} %get-tuple-element.142) | copy-start | bytes 1966084
  410.9 8.8 %collective-permute-start.50 = (bf16[128,1280]{1,0:T(8,128)(2,1)}, bf16[128,1280]{1,0:T(8,128)(2,1)S(1)}, u32[]{:S(2)}, u32[]{:S(2)}) collective-permute-start(bf16[128,1280]{1,0:T(8,128)(2,1)} %get-tuple-element.154), channel_id=1, source_target_pairs={{0,38},{1,3},{8,46},{9,11},{16,54},{17,19},{24,62},{25,27},{2,0},{... | collective-permute-start | bytes 983048 | tf_op jit(solution)/shard_map/ppermute | solution.py:34
  415.0 14.7 %copy-start.23 = (f32[128,1280]{1,0:T(8,128)S(1)}, f32[128,1280]{1,0:T(8,128)}, u32[]{:S(2)}) copy-start(f32[128,1280]{1,0:T(8,128)} %get-tuple-element.153) | copy-start | bytes 1966084
  415.0 11.2 %collective-permute-start.40 = (bf16[128,1280]{1,0:T(8,128)(2,1)S(1)}, bf16[128,1280]{1,0:T(8,128)(2,1)S(1)}, u32[]{:S(2)}, u32[]{:S(2)}) collective-permute-start(bf16[128,1280]{1,0:T(8,128)(2,1)S(1)} %add_convert_fusion.3), channel_id=1, source_target_pairs={{0,38},{1,3},{8,46},{9,11},{16,54},{17,19},{24,62},{25,27},{2,0},{... | collective-permute-start | bytes 983048 | tf_op jit(solution)/shard_map/ppermute | solution.py:34
  415.1 13.0 %collective-permute-start.52 = (bf16[128,1280]{1,0:T(8,128)(2,1)}, bf16[128,1280]{1,0:T(8,128)(2,1)S(1)}, u32[]{:S(2)}, u32[]{:S(2)}) collective-permute-start(bf16[128,1280]{1,0:T(8,128)(2,1)} %get-tuple-element.156), channel_id=1, source_target_pairs={{0,2},{1,39},{8,10},{9,47},{16,18},{17,55},{24,26},{25,63},{2,4},{... | collective-permute-start | bytes 983048 | tf_op jit(solution)/shard_map/ppermute | solution.py:34
  420.8 8.9 %collective-permute-start.51 = (bf16[128,1280]{1,0:T(8,128)(2,1)S(1)}, bf16[128,1280]{1,0:T(8,128)(2,1)S(1)}, u32[]{:S(2)}, u32[]{:S(2)}) collective-permute-start(bf16[128,1280]{1,0:T(8,128)(2,1)S(1)} %add_convert_fusion.1), channel_id=1, source_target_pairs={{0,38},{1,3},{8,46},{9,11},{16,54},{17,19},{24,62},{25,27},{2,0},{... | collective-permute-start | bytes 983048 | tf_op jit(solution)/shard_map/ppermute | solution.py:34
  426.3 4.4 collective-permute-start.55
  434.6 19.2 %copy-start.6 = (bf16[288,2560]{1,0:T(8,128)(2,1)S(1)}, bf16[288,2560]{1,0:T(8,128)(2,1)}, u32[]{:S(2)}) copy-start(bf16[288,2560]{1,0:T(8,128)(2,1)} %choose.10) | copy-start | bytes 4423684
  434.6 19.2 %copy-start.10 = (f32[96,1280]{1,0:T(8,128)S(1)}, f32[96,1280]{1,0:T(8,128)}, u32[]{:S(2)}) copy-start(f32[96,1280]{1,0:T(8,128)} %convert_add_fusion.1.refs_0_) | copy-start | bytes 1474564
  434.6 10.7 %collective-permute-start.16 = (bf16[96,1280]{1,0:T(8,128)(2,1)S(1)}, bf16[96,1280]{1,0:T(8,128)(2,1)S(1)}, u32[]{:S(2)}, u32[]{:S(2)}) collective-permute-start(bf16[96,1280]{1,0:T(8,128)(2,1)S(1)} %get-tuple-element.98), channel_id=1, source_target_pairs={{0,2},{1,3},{8,10},{9,11},{16,18},{17,19},{24,26},{25,27},{2,0},{3... | collective-permute-start | bytes 737288 | tf_op jit(solution)/shard_map/cond/branch_1_fun/ppermute | solution.py:34
  436.9 15.8 %collective-permute-start.17 = (bf16[96,1280]{1,0:T(8,128)(2,1)S(1)}, bf16[96,1280]{1,0:T(8,128)(2,1)}, u32[]{:S(2)}, u32[]{:S(2)}) collective-permute-start(bf16[96,1280]{1,0:T(8,128)(2,1)S(1)} %get-tuple-element.99), channel_id=1, source_target_pairs={{0,34},{1,35},{8,42},{9,43},{16,50},{17,51},{24,58},{25,59},{2,32}... | collective-permute-start | bytes 737288 | tf_op jit(solution)/shard_map/cond/branch_1_fun/ppermute | solution.py:34
  (2 other events, 1.6 us)
Sparse Core Ops, SparseCore 0:
  10.6 109.8 all-gather.2
  223.1 27.6 reduce-scatter.2
  303.5 27.8 reduce-scatter.4

commit v2 on v0

--- a/solution.py
+++ b/solution.py
@@ -15,8 +15,7 @@
 learn_rate = 0.003
 adam_eps = 1e-08
 
-G_CHUNKS = 1
-R_CHUNKS = 1
+G_CHUNKS = 2
 
 
 def flat_index(y, z, x, c):
@@ -100,6 +99,32 @@
     )(*arrays, *earlier)
 
 
+def mark_kernel(tokens, meta, out):
+    width = tokens.shape[1]
+    out[:, :width] = tokens[...]
+    left = meta[...]
+    total = None
+    for turn in range(3):
+        part = left.astype(jnp.bfloat16).astype(jnp.float32)
+        left = left - part
+        part = pltpu.roll(part, 16 * turn, 1) if turn else part
+        total = part if total is None else total + part
+    out[:, width:] = total.astype(jnp.bfloat16)
+
+
+def mark(tokens, meta):
+    rows, width = tokens.shape
+    return pl.pallas_call(
+        mark_kernel,
+        in_specs=[pl.BlockSpec(memory_space=pltpu.VMEM)] * 2,
+        out_specs=pl.BlockSpec(memory_space=pltpu.VMEM),
+        out_shape=jax.ShapeDtypeStruct((rows, width + 128), jnp.bfloat16),
+        compiler_params=params(60),
+        cost_estimate=LIGHT,
+        name="mark",
+    )(tokens, meta)
+
+
 def choose_kernel(wanted, other, own, *refs):
     @pl.when(wanted[0] == 1)
     def _():
@@ -143,34 +168,45 @@
     )(*blocks, *earlier)
 
 
-def plan_kernel(cap, top, ids_here, m0, m1, m2, m3, slot_ref, weight_ref):
-    rows = m0.shape[1]
+def plan_kernel(cap, top, ids_here, m0, m1, m2, m3, *refs):
+    slot_ref, weight_ref = refs[-2:]
+    rows = m0.shape[0]
     before = lax.broadcasted_iota(jnp.int32, (rows, rows), 0)
     after = lax.broadcasted_iota(jnp.int32, (rows, rows), 1)
     earlier = (before < after).astype(jnp.float32).astype(jnp.bfloat16)
     wanted = ids_here[...]
-    for s, meta in enumerate((m0, m1, m2, m3)):
+    for s, block in enumerate((m0, m1, m2, m3)):
+        meta = block[...].astype(jnp.float32).T
+        scale = meta[8:16, :] + meta[24:32, :] + meta[40:48, :]
         named = jnp.zeros(wanted.shape, jnp.float32)
         weight = jnp.zeros(wanted.shape, jnp.float32)
         for k in range(top):
             same = (meta[k : k + 1, :] == wanted).astype(jnp.float32)
             named = named + same
-            weight = weight + same * meta[8 + k : 9 + k, :]
+            weight = weight + same * scale[k : k + 1, :]
         rank = jnp.dot(named.astype(jnp.bfloat16), earlier, preferred_element_type=jnp.float32)
         slot = jnp.where(named > 0.5, rank + float(s * cap), -1.0)
         slot_ref[:, s * rows : (s + 1) * rows] = slot
         weight_ref[:, s * rows : (s + 1) * rows] = weight
 
 
-def make_plan(cap, top, ids_here, metas):
-    rows = metas[0].shape[1]
+def make_plan(cap, top, ids_here, parts, *earlier):
+    rows, width = parts[0].shape
+    last = width // 128 - 1
     out = jax.ShapeDtypeStruct((ids_here.shape[0], 4 * rows), jnp.float32)
+    whole = pl.BlockSpec(out.shape, lambda i: (0, 0))
     return pl.pallas_call(
         lambda *refs: plan_kernel(cap, top, *refs),
+        grid=(1,),
+        in_specs=[pl.BlockSpec(ids_here.shape, lambda i: (0, 0))]
+        + [pl.BlockSpec((rows, 128), lambda i: (0, last)) for _ in parts]
+        + [pl.BlockSpec(memory_space=pl.ANY) for _ in earlier],
+        out_specs=(whole, whole),
         out_shape=(out, out),
-        compiler_params=params(16),
+        compiler_params=params(60, "arbitrary"),
+        cost_estimate=LIGHT,
         name="plan",
-    )(ids_here, *metas)
+    )(ids_here, *parts, *earlier)
 
 
 def select_kernel(scaled, slots, weights, t0, t1, t2, t3, *refs):
@@ -199,11 +235,12 @@
         outs[-1][...] = rows.astype(jnp.bfloat16).reshape(8, block, -1)
 
 
-def select_rows(scaled, cap, plan, parts, *earlier):
+def select_rows(scaled, cap, plan, parts, first, width, *earlier):
     slots, weights = plan
-    rows, width = parts[0].shape
+    rows = parts[0].shape[0]
     block = 4 * cap
-    tile = 512
+    tile = 256 if width % 512 else 512
+    offset = first // tile
     whole = pl.BlockSpec(slots.shape, lambda j: (0, 0))
     if scaled:
         out_spec = (pl.BlockSpec((2 * block, tile), lambda j: (0, j)),) * 4
@@ -215,7 +252,7 @@
         lambda *refs: select_kernel(scaled, *refs),
         grid=(width // tile,),
         in_specs=[whole, whole]
-        + [pl.BlockSpec((rows, tile), lambda j: (0, j)) for _ in range(4)]
+        + [pl.BlockSpec((rows, tile), lambda j: (0, j + offset)) for _ in range(4)]
         + [pl.BlockSpec(memory_space=pl.ANY) for _ in earlier],
         out_specs=out_spec,
         out_shape=out_shape,
@@ -230,7 +267,7 @@
 
 
 def hidden_kernel(count, where, *refs):
-    xs, (gate_w, up_w, _, fixed, turned, held) = refs[:count], refs[count:]
+    xs, (gate_w, up_w), (fixed, turned, held) = refs[:count], refs[count : count + 2], refs[-3:]
     step, tile = pl.program_id(0), gate_w.shape[1]
     steps, features = held.shape[0], fixed.shape[1]
     gate, up, first = None, None, 0
@@ -272,21 +309,22 @@
         in_specs=[pl.BlockSpec(memory_space=pltpu.SMEM)]
         + [pl.BlockSpec(x.shape, lambda j: (0, 0, 0)) for x in xs]
         + [pl.BlockSpec((depth, tile), lambda j: (0, j)) for _ in range(2)]
-        + [pl.BlockSpec(memory_space=pl.ANY)],
+        + [pl.BlockSpec(memory_space=pl.ANY) for _ in earlier],
         out_specs=(pl.BlockSpec((count, features), lambda j: (0, 0)),) * 2,
         out_shape=(jax.ShapeDtypeStruct((count, features), jnp.bfloat16),) * 2,
         scratch_shapes=[pltpu.VMEM((steps, count, tile), jnp.bfloat16)],
         compiler_params=params(60, "arbitrary"),
         name="hidden",
-    )(where, *xs, gate_weight, up_weight, earlier)
-
-
-def down_kernel(hidden, down, out):
+    )(where, *xs, gate_weight, up_weight, *earlier)
+
+
+def down_kernel(hidden, down, *refs):
+    out = refs[-1]
     rows = jnp.dot(hidden[...], down[...], preferred_element_type=jnp.float32)
     out[...] = rows.astype(jnp.bfloat16).reshape(out.shape)
 
 
-def down_rows(hidden, down, cap, first, width):
+def down_rows(hidden, down, cap, first, width, *earlier):
     tile = 256 if width % 512 else 512
     offset = first // tile
     block = 4 * cap
@@ -294,16 +332,17 @@
         down_kernel,
         grid=(width // tile,),
         in_specs=[pl.BlockSpec(hidden.shape, lambda j: (0, 0))]
-        + [pl.BlockSpec((down.shape[0], tile), lambda j: (0, j + offset))],
+        + [pl.BlockSpec((down.shape[0], tile), lambda j: (0, j + offset))]
+        + [pl.BlockSpec(memory_space=pl.ANY) for _ in earlier],
         out_specs=pl.BlockSpec((8, block, tile), lambda j: (0, 0, j)),
         out_shape=jax.ShapeDtypeStruct((8, block, width), jnp.bfloat16),
         compiler_params=params(60, "arbitrary"),
         name="down",
-    )(hidden, down)
+    )(hidden, down, *earlier)
 
 
 def grad_kernel(where, hidden, *refs):
-    rows, outs, turned = refs[:5], refs[5:9], refs[9]
+    rows, outs, turned = refs[:5], refs[-5:-1], refs[-1]
     block = rows[0].shape[0]
 
     @pl.when(pl.program_id(0) == 0)
@@ -321,7 +360,7 @@
         out[...] = grad[k * quarter : (k + 1) * quarter, :]
 
 
-def grad_blocks(where, hidden, rows, first, width):
+def grad_blocks(where, hidden, rows, first, width, *earlier):
     block = rows[0].shape[0] // 2
     tile = 256 if width % 512 else 512
     offset = first // tile
@@ -336,13 +375,14 @@
             pl.BlockSpec(hidden.shape, lambda j: (0, 0)),
         ]
         + [pl.BlockSpec((block, tile), lambda j: (0, j + offset)) for _ in range(4)]
-        + [pl.BlockSpec((4 * block, tile), lambda j: (0, j + offset))],
+        + [pl.BlockSpec((4 * block, tile), lambda j: (0, j + offset))]
+        + [pl.BlockSpec(memory_space=pl.ANY) for _ in earlier],
         out_specs=(spec,) * 4,
         out_shape=(out,) * 4,
         scratch_shapes=[pltpu.VMEM(hidden.shape[::-1], jnp.bfloat16)],
         compiler_params=params(60, "arbitrary"),
         name="grad",
-    )(where, hidden, *rows)
+    )(where, hidden, *rows, *earlier)
 
 
 def combine_kernel(slots, weights, rows, o0, o1, o2, o3, high, low):
@@ -461,54 +501,49 @@
     ids = jnp.arange(experts, dtype=jnp.int32)
     here = jnp.sum(jnp.where(placement[None, :] == held_at[:, None], ids[None, :], 0), axis=1)
     here = jnp.broadcast_to(here.astype(jnp.float32)[:, None], (16, tok_rows))
-    pad = jnp.zeros((8 - top, tok_rows), jnp.float32)
-    meta = jnp.concatenate([expert_ids.T.astype(jnp.float32), pad, route_weight.T, pad], axis=0)
-
-    plan = make_plan(cap, top, here, z_gather(meta))
-    x_parts = z_gather(tokens)
+    numbers = jnp.pad(expert_ids.astype(jnp.float32), ((0, 0), (0, 128 - top)))
+    meta = numbers + jnp.pad(route_weight, ((0, 0), (8, 120 - top)))
+
+    x_parts = z_gather(mark(tokens, meta))
     state = hold((down_weight[0], first_moment[0], second_moment[0]))
     far_state = swap(state, x=1)
-    x_send = select_rows(False, cap, plan, x_parts, far_state)
+    plan = make_plan(cap, top, here, x_parts, far_state)
+    x_send = select_rows(False, cap, plan, x_parts, 0, width)
     x_rows = plane_exchange(x_send)
-    g_parts = z_gather(hold((out_grad,), x_send))
+    g_parts = z_gather(hold((out_grad,), plan[0]))
     state = choose(bits[3], far_state, state, x_send)
-    state_cores = choose(bits[0], swap(state, c=1), state, g_parts[1], g_parts[2])
-    state = choose(bits[1], swap(state_cores, zl=1), state_cores)
-    state_far = swap(state, zl=2)
-
-    g_send = select_rows(True, cap, plan, g_parts, x_rows, state_cores)
+    state_cores = choose(bits[0], swap(state, c=1), state, *g_parts[2:])
+    state_far = swap(state_cores, zl=2)
+
+    g_send = select_rows(True, cap, plan, g_parts, 0, width, x_rows, state_cores)
     g_rows = plane_permute(g_send)
 
-    down_full = lax.all_gather(down_weight[0], ("y", "zh"), axis=0, tiled=True)
-
-    hidden, turned = hidden_rows(where, [x_rows], gate_weight[0], up_weight[0], g_send[3])
-
-    chunk = width // R_CHUNKS
-    r_sends = [down_rows(hidden, down_full, cap, i * chunk, chunk) for i in range(R_CHUNKS)]
-    returned = [plane_exchange(r) for r in r_sends]
-
-    g_rows = (*g_rows, core_permute(g_rows, r_sends[0], state))
-    state = jnp.split(choose(bits[2], state_far, state, r_sends[0]), 3, axis=0)
-
-    halves = []
-    chunk = width // G_CHUNKS
+    down_full = lax.all_gather(hold((down_weight[0],), plan[0]), ("y", "zh"), axis=0, tiled=True)
+
+    hidden, turned = hidden_rows(where, [x_rows], gate_weight[0], up_weight[0], g_send[3:])
+    r_send = down_rows(hidden, down_full, cap, 0, width)
+    returned = plane_exchange(r_send)
+    state_far = choose(bits[2], state_far, state_cores, r_send)
+    state = choose(bits[1], swap(state_far, zl=1), state_far)
+
+    g_rows = (*g_rows, core_permute(g_rows, state_far))
+    grads, blocks, chunk = [], (r_send,), width // G_CHUNKS
     for i in range(G_CHUNKS):
-        blocks = grad_blocks(where, turned, g_rows, i * chunk, chunk)
+        blocks = grad_blocks(where, turned, g_rows, i * chunk, chunk, blocks[0])
         blocks = [blocks[0]] + [y_move(blocks[k], k) for k in (1, 2, 3)]
-        halves.append(sum_blocks(blocks, returned[0]))
-    total = jnp.concatenate(halves, axis=1)
-    total = jnp.where(bits[0][0] == 1, swap(total, c=1), total)
-    rows = total.shape[0] // 2
-    mine, theirs = lax.switch(
-        jump,
-        [lambda a, b, m=m: (relocate(a, m), relocate(b, m, True)) for m in jumps],
-        total[:rows],
-        total[rows:],
-    )
-    grad = mine.astype(jnp.float32) + theirs.astype(jnp.float32)
-    new_state = adam(grad, *state)
-
-    layer_out = jnp.concatenate([z_return(*combine_rows(plan, r)) for r in returned], axis=1)
+        total = sum_blocks(blocks, state, *((grads[-1], returned) if grads else ()))
+        total = choose(bits[0], swap(total, c=1), total)
+        rows = total.shape[0] // 2
+        mine, theirs = lax.switch(
+            jump,
+            [lambda a, b, m=m: (relocate(a, m), relocate(b, m, True)) for m in jumps],
+            total[:rows],
+            total[rows:],
+        )
+        grads.append(mine.astype(jnp.float32) + theirs.astype(jnp.float32))
+    new_state = adam(jnp.concatenate(grads, axis=1), *jnp.split(state, 3, axis=0))
+
+    layer_out = z_return(*combine_rows(plan, returned))
     return (layer_out, *new_state)
 
 

time: 325 us -> 386 us (1.19)
  waiting for transfers between devices: 158 us -> 175 us
  Pallas kernels: 78.3 us -> 93.5 us
  loops' own time: 0.04 us -> 12.9 us
  starting transfers between devices: 57.9 us -> 67.6 us
  local copies, waits for them, and re-layouts: 6.73 us -> 11.9 us
    ppermute x26 -> x29, waiting for transfers between devices: 142 us -> 175 us  [permute(): return lax.ppermute(array, AXES, pairs)]
    all_to_all x2, waiting for transfers between devices: 15.9 us -> 0.01 us  [plane_exchange(): lax.all_to_all(rows, ('x', 'c'), split_axis=0, concat_axis=0, tiled=True)]
    unnamed x1 -> x2, loops' own time: 0.04 us -> 12.9 us
    ppermute x26 -> x29, starting transfers between devices: 40.9 us -> 51.9 us  [permute(): return lax.ppermute(array, AXES, pairs)]
    pallas_call x1 -> x2, Pallas kernels: 8.73 us -> 13.5 us  [grad_blocks(): pl.pallas_call(grad_kernel, grid=(width // tile,), in_specs=[pl.BlockSpec...]
    pallas_call x4 -> x6, Pallas kernels: 12.5 us -> 16.4 us  [choose(): pl.pallas_call(choose_kernel, in_specs=[pl.BlockSpec(memory_space=pltpu.S...]
    unnamed x43 -> x55, local copies, waits for them, and re-layouts: 6.59 us -> 8.82 us
    pallas_call x3 -> x4, Pallas kernels: 8.53 us -> 10.2 us  [hold(): pl.pallas_call(lambda *refs: hold_kernel(len(arrays), start, *refs), in_s...]
  transfers between devices with their start and end apart: 29 -> 32, of which waited for: 14 -> 12; matrix products, arithmetic and copies ran while one was open for 2% -> 2% of each run, Pallas kernels for 24% -> 21%
where the time goes in v2:
time: 386 us; the launch traced here: 383 us
  waiting for transfers between devices  175 us (45%)
  Pallas kernels  93.5 us (24%)
  starting transfers between devices  67.6 us (18%)
  between operations  15.2 us (4%)
  loops' own time  12.9 us (3%)
  local copies, waits for them, and re-layouts  11.9 us (3%)
  other arithmetic  7.42 us (2%)
    ppermute x29, waiting for transfers between devices, permute(): return lax.ppermute(array, AXES, pairs)  175 us
    ppermute x29, starting transfers between devices, permute(): return lax.ppermute(array, AXES, pairs)  51.9 us
    pallas_call x6, Pallas kernels, choose(): pl.pallas_call(choose_kernel, in_specs=[pl.BlockSpec(memory_space=pltpu.S...  16.4 us
    all_to_all x2, starting transfers between devices, plane_exchange(): lax.all_to_all(rows, ('x', 'c'), split_axis=0, concat_axis=0, tiled=True)  15.6 us
    pallas_call x2, Pallas kernels, select_rows(): pl.pallas_call(lambda *refs: select_kernel(scaled, *refs), grid=(width //...  13.8 us
    pallas_call x1, Pallas kernels, hidden_rows(): pl.pallas_call(lambda *refs: hidden_kernel(len(xs), *refs), grid=(steps,)...  13.7 us
    pallas_call x2, Pallas kernels, grad_blocks(): pl.pallas_call(grad_kernel, grid=(width // tile,), in_specs=[pl.BlockSpec...  13.5 us
    unnamed x2, loops' own time  12.9 us
  transfers between devices with their start and end apart: 32, of which 12 were waited for; matrix products, arithmetic and copies ran while one was open for 2% of the time, Pallas kernels for 21%

profile of v2, /device:TPU:1, one launch (start us, length us, event | category | flops | bytes accessed | tf_op | source)
XLA Modules:
  0.0 383.1 jit_solution(18203286644082674478)
XLA Ops:
  7.2 2.6 hold.4.own
  9.8 2.0 collective-permute-start.33
  12.8 2.0 mark.1.refs_1_.refs_2_
  14.8 5.6 %collective-permute-start.30 = (bf16[128,2688]{1,0:T(8,128)(2,1)}, bf16[128,2688]{1,0:T(8,128)(2,1)S(1)}, u32[]{:S(2)}, u32[]{:S(2)}) collective-permute-start(bf16[128,2688]{1,0:T(8,128)(2,1)} %mark.1.refs_1_.refs_2_), channel_id=1, source_target_pairs={{0,2},{1,39},{8,10},{9,47},{16,18},{17,55},{24,26},{25,63},{2,4},{... | collective-permute-start | bytes 2064392 | tf_op jit(solution)/shard_map/ppermute | solution.py:33
  20.4 14.1 %collective-permute-done.30.refs_2_.refs_3_ = bf16[128,2688]{1,0:T(8,128)(2,1)S(1)} collective-permute-done((bf16[128,2688]{1,0:T(8,128)(2,1)}, bf16[128,2688]{1,0:T(8,128)(2,1)S(1)}, u32[]{:S(2)}, u32[]{:S(2)}) %collective-permute-start.30) | collective-permute-done | bytes 688160 | tf_op jit(solution)/shard_map/ppermute | solution.py:33
  34.5 3.3 collective-permute-start.32
  38.2 7.6 %collective-permute-done.32.refs_4_.refs_5_ = bf16[128,2688]{1,0:T(8,128)(2,1)S(1)} collective-permute-done((bf16[128,2688]{1,0:T(8,128)(2,1)S(1)}, bf16[128,2688]{1,0:T(8,128)(2,1)S(1)}, u32[]{:S(2)}, u32[]{:S(2)}) %collective-permute-start.32) | collective-permute-done | bytes 688160 | tf_op jit(solution)/shard_map/ppermute | solution.py:33
  47.1 1.7 plan.1
  48.8 1.8 hold.6
  50.6 7.1 %select.94.refs_0_ = bf16[8,112,2560]{2,1,0:T(8,128)(2,1)} custom-call(f32[16,512]{1,0:T(8,128)} %get-tuple-element.140.refs_0_.refs_1_.slots, f32[16,512]{1,0:T(8,128)} %get-tuple-element.141.refs_1_.weights, bf16[128,2688]{1,0:T(8,128)(2,1)} %mark.1.refs_1_.refs_2_, bf16[128,2688]{1,0:T(8,128)(2,1)} %copy-done.6, bf16[128,2688]{1,0:T(8,128)(2,1)} %copy-done.7, ...), custom_call_target="tpu_custom_call" | custom-call | flops 1 | bytes 1 | tf_op jit(solution)/shard_map/select/pallas_call | solution.py:251
  57.8 7.5 %all-to-all-start = ((bf16[8,112,2560]{2,1,0:T(8,128)(2,1)}), bf16[8,112,2560]{2,1,0:T(8,128)(2,1)}, u32[]{:S(2)}, u32[]{:S(2)}) async-start(bf16[8,112,2560]{2,1,0:T(8,128)(2,1)} %select.94.refs_0_), calls=%async_computation | async-start | bytes 9175040 | tf_op jit(solution)/shard_map/all_to_all | solution.py:450
  65.9 3.2 choose.6.own
  69.3 2.0 hold.5.refs_2_
  71.3 2.2 collective-permute-start.34
  73.5 20.2 %collective-permute-done.34.refs_3_ = bf16[128,2560]{1,0:T(8,128)(2,1)S(1)} collective-permute-done((bf16[128,2560]{1,0:T(8,128)(2,1)}, bf16[128,2560]{1,0:T(8,128)(2,1)S(1)}, u32[]{:S(2)}, u32[]{:S(2)}) %collective-permute-start.34) | collective-permute-done | bytes 655392 | tf_op jit(solution)/shard_map/ppermute | solution.py:33
  93.7 2.3 collective-permute-start.36
  96.5 49.2 %collective-permute-done.36.refs_1_.refs_5_ = bf16[128,2560]{1,0:T(8,128)(2,1)S(1)} collective-permute-done((bf16[128,2560]{1,0:T(8,128)(2,1)S(1)}, bf16[128,2560]{1,0:T(8,128)(2,1)S(1)}, u32[]{:S(2)}, u32[]{:S(2)}) %collective-permute-start.36) | collective-permute-done | bytes 655392 | tf_op jit(solution)/shard_map/ppermute | solution.py:33
  145.7 0.8 copy-done.10
  146.5 1.1 copy-done.12
  147.6 3.1 choose.7.refs_7_.own
  150.7 6.7 %select_scaled.1 = (bf16[224,2560]{1,0:T(8,128)(2,1)}, bf16[224,2560]{1,0:T(8,128)(2,1)}, bf16[224,2560]{1,0:T(8,128)(2,1)}, bf16[224,2560]{1,0:T(8,128)(2,1)}) custom-call(f32[16,512]{1,0:T(8,128)} %get-tuple-element.140.refs_0_.refs_1_.slots, f32[16,512]{1,0:T(8,128)} %get-tuple-element.141.refs_1_.weights, bf16[128,2560]{1,0:T(8,128)(2,1)} %hold.5.refs_2_, ...), custom_call_target="tpu_custom_call" | custom-call | flops 1 | bytes 1 | tf_op jit(solution)/shard_map/select_scaled/pallas_call | solution.py:251
  157.5 3.8 collective-permute-start.44
  162.1 13.7 %hidden.1 = (bf16[896,768]{1,0:T(8,128)(2,1)}, bf16[896,768]{1,0:T(8,128)(2,1)}) custom-call(s32[4]{0:T(128)} %pad_add_fusion.2.refs_0_.where, bf16[8,112,2560]{2,1,0:T(8,128)(2,1)} %all-to-all-done.refs_6_.refs_1_, bf16[2560,768]{1,0:T(8,128)(2,1)} %bitcast.20, bf16[2560,768]{1,0:T(8,128)(2,1)} %bitcast.21, bf16[224,2560]{1,0:T(8,128)(2,1)} %get-tuple-element.142.refs_4_), custom_call_target="tpu_custom_call" | custom-call | tf_op jit(solution)/shard_map/hidden/pallas_call | solution.py:306
  175.8 8.2 %down.1.refs_0_.refs_5_ = bf16[8,112,2560]{2,1,0:T(8,128)(2,1)} custom-call(bf16[896,768]{1,0:T(8,128)(2,1)} %get-tuple-element.143.hidden, bf16[768,2560]{1,0:T(8,128)(2,1)} %all-gather.2.cloned.1.call-done.down), custom_call_target="tpu_custom_call" | custom-call | tf_op jit(solution)/shard_map/down/pallas_call | solution.py:331
  184.0 29.5 %collective-permute-done.41.other = bf16[288,2560]{1,0:T(8,128)(2,1)} collective-permute-done((bf16[288,2560]{1,0:T(8,128)(2,1)}, bf16[288,2560]{1,0:T(8,128)(2,1)}, u32[]{:S(2)}, u32[]{:S(2)}) %collective-permute-start.41) | collective-permute-done | bytes 1474592 | tf_op jit(solution)/shard_map/ppermute | solution.py:33
  213.5 3.1 choose.8.own.refs_4_
  216.6 1.0 copy-done.2
  218.0 3.8 hold.7
  222.3 8.1 %all-to-all-start.1 = ((bf16[8,112,2560]{2,1,0:T(8,128)(2,1)}), bf16[8,112,2560]{2,1,0:T(8,128)(2,1)}, u32[]{:S(2)}, u32[]{:S(2)}) async-start(bf16[8,112,2560]{2,1,0:T(8,128)(2,1)} %down.1.refs_0_.refs_5_), calls=%async_computation.1 | async-start | bytes 9175040 | tf_op jit(solution)/shard_map/all_to_all | solution.py:450
  230.4 6.7 %grad.2 = (bf16[192,1280]{1,0:T(8,128)(2,1)}, bf16[192,1280]{1,0:T(8,128)(2,1)}, bf16[192,1280]{1,0:T(8,128)(2,1)}, bf16[192,1280]{1,0:T(8,128)(2,1)}) custom-call(s32[4]{0:T(128)} %pad_add_fusion.2.refs_0_.where, bf16[896,768]{1,0:T(8,128)(2,1)} %get-tuple-element.148.hidden, bf16[224,2560]{1,0:T(8,128)(2,1)} %get-tuple-element.149.refs_0_, ...), custom_call_target="tpu_custom_call" | custom-call | tf_op jit(solution)/shard_map/grad/pallas_call | solution.py:370
  237.1 1.3 collective-permute-start.47
  238.4 2.7 collective-permute-start.48
  241.1 1.1 collective-permute-start.49
  242.2 22.1 %collective-permute-done.42.other = bf16[288,2560]{1,0:T(8,128)(2,1)S(1)} collective-permute-done((bf16[288,2560]{1,0:T(8,128)(2,1)S(1)}, bf16[288,2560]{1,0:T(8,128)(2,1)S(1)}, u32[]{:S(2)}, u32[]{:S(2)}) %collective-permute-start.42) | collective-permute-done | bytes 1474592 | tf_op jit(solution)/shard_map/ppermute | solution.py:33
  264.3 1.1 copy-done.11
  265.5 3.1 choose.9.refs_0_
  269.5 2.5 sum.2.own
  272.7 6.7 %grad.3 = (bf16[192,1280]{1,0:T(8,128)(2,1)}, bf16[192,1280]{1,0:T(8,128)(2,1)}, bf16[192,1280]{1,0:T(8,128)(2,1)}, bf16[192,1280]{1,0:T(8,128)(2,1)}) custom-call(s32[4]{0:T(128)} %pad_add_fusion.2.refs_0_.where, bf16[896,768]{1,0:T(8,128)(2,1)} %get-tuple-element.148.hidden, bf16[224,2560]{1,0:T(8,128)(2,1)} %get-tuple-element.149.refs_0_, ...), custom_call_target="tpu_custom_call" | custom-call | tf_op jit(solution)/shard_map/grad/pallas_call | solution.py:370
  279.5 1.2 collective-permute-start.51
  280.7 2.7 collective-permute-start.52
  283.4 1.1 collective-permute-start.53
  285.3 2.0 choose.10
  287.3 1.1 fusion.9
  288.4 27.2 %conditional.8 = (bf16[96,1280]{1,0:T(8,128)(2,1)S(1)}, bf16[96,1280]{1,0:T(8,128)(2,1)}) conditional(s32[]{:T(128)} %clamp.4, (bf16[96,1280]{1,0:T(8,128)(2,1)S(1)}, bf16[96,1280]{1,0:T(8,128)(2,1)S(1)}) %tuple.140, (bf16[96,1280]{1,0:T(8,128)(2,1)S(1)}, bf16[96,1280]{1,0:T(8,128)(2,1)S(1)}) %fusion.9, ...), branch_computations={%region_1.2_spmd, %region_2.3_spmd, %region_3.4_spmd, %region_4.5_... | conditional | bytes 2457696
  301.2 2.7 collective-permute-start.13
  303.9 2.8 collective-permute-start.14
  306.7 6.3 %collective-permute-done.13 = bf16[96,1280]{1,0:T(8,128)(2,1)S(1)} collective-permute-done((bf16[96,1280]{1,0:T(8,128)(2,1)S(1)}, bf16[96,1280]{1,0:T(8,128)(2,1)S(1)}, u32[]{:S(2)}, u32[]{:S(2)}) %collective-permute-start.13) | collective-permute-done | bytes 245792 | tf_op jit(solution)/shard_map/cond/branch_7_fun/ppermute | solution.py:33
  313.0 2.6 collective-permute-done.14
  315.6 1.8 convert_add_fusion.1.refs_1_
  318.5 2.5 sum.3.own
  321.0 4.6 %collective-permute-start.54 = (bf16[192,1280]{1,0:T(8,128)(2,1)}, bf16[192,1280]{1,0:T(8,128)(2,1)S(1)}, u32[]{:S(2)}, u32[]{:S(2)}) collective-permute-start(bf16[192,1280]{1,0:T(8,128)(2,1)} %sum.3.own), channel_id=1, source_target_pairs={{0,1},{1,0},{8,9},{9,8},{16,17},{17,16},{24,25},{25,24},{2,3},{3,2... | collective-permute-start | bytes 1474568 | tf_op jit(solution)/shard_map/ppermute | solution.py:33
  325.7 9.0 %combine.1 = (f32[128,2560]{1,0:T(8,128)}, bf16[128,2560]{1,0:T(8,128)(2,1)}, bf16[128,2560]{1,0:T(8,128)(2,1)}, bf16[128,2560]{1,0:T(8,128)(2,1)}) custom-call(f32[16,512]{1,0:T(8,128)} %get-tuple-element.140.refs_0_.refs_1_.slots, f32[16,512]{1,0:T(8,128)} %get-tuple-element.141.refs_1_.weights, bf16[8,112,2560]{2,1,0:T(8,128)(2,1)} %all-to-all-done.1.rows.refs_2_), custom_call_target="tpu_custom_call" | custom-call | tf_op jit(solution)/shard_map/combine/pallas_call | solution.py:419
  335.2 2.1 collective-permute-start.40
  338.1 2.0 choose.11
  340.1 1.1 fusion.8
  341.2 21.0 %conditional.9 = (bf16[96,1280]{1,0:T(8,128)(2,1)S(1)}, bf16[96,1280]{1,0:T(8,128)(2,1)}) conditional(s32[]{:T(128)} %clamp.4, (bf16[96,1280]{1,0:T(8,128)(2,1)S(1)}, bf16[96,1280]{1,0:T(8,128)(2,1)S(1)}) %tuple.142, (bf16[96,1280]{1,0:T(8,128)(2,1)S(1)}, bf16[96,1280]{1,0:T(8,128)(2,1)S(1)}) %fusion.8, ...), branch_computations={%region_9.10_spmd, %region_10.11_spmd, %region_11.12_spmd, %region... | conditional | bytes 2457696
  342.0 3.8 %collective-permute-start.29 = (bf16[96,1280]{1,0:T(8,128)(2,1)S(1)}, bf16[96,1280]{1,0:T(8,128)(2,1)}, u32[]{:S(2)}, u32[]{:S(2)}) collective-permute-start(bf16[96,1280]{1,0:T(8,128)(2,1)S(1)} %get-tuple-element.111), channel_id=1, source_target_pairs={{0,46},{1,47},{8,38},{9,39},{16,62},{17,63},{24,54},{25,55},{2,44}... | collective-permute-start | bytes 737288 | tf_op jit(solution)/shard_map/cond/branch_7_fun/ppermute | solution.py:33
  345.9 13.8 %collective-permute-done.28 = bf16[96,1280]{1,0:T(8,128)(2,1)S(1)} collective-permute-done((bf16[96,1280]{1,0:T(8,128)(2,1)S(1)}, bf16[96,1280]{1,0:T(8,128)(2,1)S(1)}, u32[]{:S(2)}, u32[]{:S(2)}) %collective-permute-start.28) | collective-permute-done | bytes 245792 | tf_op jit(solution)/shard_map/cond/branch_7_fun/ppermute | solution.py:33
  359.7 2.5 collective-permute-done.29
  362.2 1.1 convert_add_fusion
  363.6 3.6 collective-permute-start.39
  367.1 1.7 convert_bitcast_fusion
  368.8 6.1 %collective-permute-done.39 = bf16[128,2560]{1,0:T(8,128)(2,1)S(1)} collective-permute-done((bf16[128,2560]{1,0:T(8,128)(2,1)S(1)}, bf16[128,2560]{1,0:T(8,128)(2,1)S(1)}, u32[]{:S(2)}, u32[]{:S(2)}) %collective-permute-start.39) | collective-permute-done | bytes 655392 | tf_op jit(solution)/shard_map/ppermute | solution.py:33
  375.0 1.1 add_convert_fusion
  (96 shorter events, 10.9 us)
Async XLA Ops:
  7.2 168.7 %all-gather.2.cloned.1.call-start = ((), (), s32[]{:S(2)}) async-start(), calls=%async_computation.2 | async-start | bytes 4423680 | tf_op jit(solution)/shard_map/all_gather | solution.py:521
  7.2 4.6 %copy-start.24 = (s32[128,6]{0,1:T(8,128)S(1)}, s32[128,6]{0,1:T(8,128)}, u32[]{:S(2)}) copy-start(s32[128,6]{0,1:T(8,128)} %param.28) | copy-start | bytes 9220
  7.2 4.8 %copy-start.23 = (f32[128,6]{0,1:T(8,128)S(1)}, f32[128,6]{0,1:T(8,128)}, u32[]{:S(2)}) copy-start(f32[128,6]{0,1:T(8,128)} %param.29) | copy-start | bytes 9220
  9.8 28.1 %copy-start.25 = (s32[32]{0:T(128)S(1)}, s32[32]{0:T(128)}, u32[]{:S(2)}) copy-start(s32[32]{0:T(128)} %param.30) | copy-start | bytes 388
  9.8 35.9 %collective-permute-start.33 = (bf16[288,2560]{1,0:T(8,128)(2,1)}, bf16[288,2560]{1,0:T(8,128)(2,1)S(1)}, u32[]{:S(2)}, u32[]{:S(2)}) collective-permute-start(bf16[288,2560]{1,0:T(8,128)(2,1)} %hold.4.own), channel_id=1, source_target_pairs={{0,8},{1,9},{8,0},{9,1},{16,24},{17,25},{24,16},{25,17},{2,10},{3,... | collective-permute-start | bytes 4423688 | tf_op jit(solution)/shard_map/ppermute | solution.py:33
  14.8 19.7 %collective-permute-start.30 = (bf16[128,2688]{1,0:T(8,128)(2,1)}, bf16[128,2688]{1,0:T(8,128)(2,1)S(1)}, u32[]{:S(2)}, u32[]{:S(2)}) collective-permute-start(bf16[128,2688]{1,0:T(8,128)(2,1)} %mark.1.refs_1_.refs_2_), channel_id=1, source_target_pairs={{0,2},{1,39},{8,10},{9,47},{16,18},{17,55},{24,26},{25,63},{2,4},{... | collective-permute-start | bytes 2064392 | tf_op jit(solution)/shard_map/ppermute | solution.py:33
  20.4 17.7 %collective-permute-start.31 = (bf16[128,2688]{1,0:T(8,128)(2,1)}, bf16[128,2688]{1,0:T(8,128)(2,1)S(1)}, u32[]{:S(2)}, u32[]{:S(2)}) collective-permute-start(bf16[128,2688]{1,0:T(8,128)(2,1)} %mark.1.refs_1_.refs_2_), channel_id=1, source_target_pairs={{0,38},{1,3},{8,46},{9,11},{16,54},{17,19},{24,62},{25,27},{2,0},{... | collective-permute-start | bytes 2064392 | tf_op jit(solution)/shard_map/ppermute | solution.py:33
  34.5 12.0 %copy-start.6 = (bf16[128,2688]{1,0:T(8,128)(2,1)}, bf16[128,2688]{1,0:T(8,128)(2,1)S(1)}, u32[]{:S(2)}) copy-start(bf16[128,2688]{1,0:T(8,128)(2,1)S(1)} %collective-permute-done.30.refs_2_.refs_3_) | copy-start | bytes 2064388
  34.5 11.2 %collective-permute-start.32 = (bf16[128,2688]{1,0:T(8,128)(2,1)S(1)}, bf16[128,2688]{1,0:T(8,128)(2,1)S(1)}, u32[]{:S(2)}, u32[]{:S(2)}) collective-permute-start(bf16[128,2688]{1,0:T(8,128)(2,1)S(1)} %collective-permute-done.30.refs_2_.refs_3_), channel_id=1, source_target_pairs={{0,2},{1,39},{8,10},{9,47},{16,18},{17,55},{24,26},{25,63},{2,4},{... | collective-permute-start | bytes 2064392 | tf_op jit(solution)/shard_map/ppermute | solution.py:33
  38.1 8.3 %copy-start.7 = (bf16[128,2688]{1,0:T(8,128)(2,1)}, bf16[128,2688]{1,0:T(8,128)(2,1)S(1)}, u32[]{:S(2)}) copy-start(bf16[128,2688]{1,0:T(8,128)(2,1)S(1)} %collective-permute-done.31.refs_3_.refs_4_) | copy-start | bytes 2064388
  45.7 0.8 copy-start.8
  45.7 1.4 copy-start.4
  57.8 92.9 %all-to-all-start = ((bf16[8,112,2560]{2,1,0:T(8,128)(2,1)}), bf16[8,112,2560]{2,1,0:T(8,128)(2,1)}, u32[]{:S(2)}, u32[]{:S(2)}) async-start(bf16[8,112,2560]{2,1,0:T(8,128)(2,1)} %select.94.refs_0_), calls=%async_computation | async-start | bytes 9175040 | tf_op jit(solution)/shard_map/all_to_all | solution.py:450
  69.1 76.5 %collective-permute-start.37 = (bf16[288,2560]{1,0:T(8,128)(2,1)}, bf16[288,2560]{1,0:T(8,128)(2,1)S(1)}, u32[]{:S(2)}, u32[]{:S(2)}) collective-permute-start(bf16[288,2560]{1,0:T(8,128)(2,1)} %choose.6.own), channel_id=1, source_target_pairs={{0,1},{1,0},{8,9},{9,8},{16,17},{17,16},{24,25},{25,24},{2,3},{3,2... | collective-permute-start | bytes 4423688 | tf_op jit(solution)/shard_map/ppermute | solution.py:33
  71.3 22.4 %collective-permute-start.34 = (bf16[128,2560]{1,0:T(8,128)(2,1)}, bf16[128,2560]{1,0:T(8,128)(2,1)S(1)}, u32[]{:S(2)}, u32[]{:S(2)}) collective-permute-start(bf16[128,2560]{1,0:T(8,128)(2,1)} %hold.5.refs_2_), channel_id=1, source_target_pairs={{0,2},{1,39},{8,10},{9,47},{16,18},{17,55},{24,26},{25,63},{2,4},{... | collective-permute-start | bytes 1966088 | tf_op jit(solution)/shard_map/ppermute | solution.py:33
  73.5 23.0 %collective-permute-start.35 = (bf16[128,2560]{1,0:T(8,128)(2,1)}, bf16[128,2560]{1,0:T(8,128)(2,1)S(1)}, u32[]{:S(2)}, u32[]{:S(2)}) collective-permute-start(bf16[128,2560]{1,0:T(8,128)(2,1)} %hold.5.refs_2_), channel_id=1, source_target_pairs={{0,38},{1,3},{8,46},{9,11},{16,54},{17,19},{24,62},{25,27},{2,0},{... | collective-permute-start | bytes 1966088 | tf_op jit(solution)/shard_map/ppermute | solution.py:33
  93.7 57.0 %copy-start.14 = (bf16[128,2560]{1,0:T(8,128)(2,1)}, bf16[128,2560]{1,0:T(8,128)(2,1)S(1)}, u32[]{:S(2)}) copy-start(bf16[128,2560]{1,0:T(8,128)(2,1)S(1)} %collective-permute-done.34.refs_3_) | copy-start | bytes 1966084
  93.7 52.0 %collective-permute-start.36 = (bf16[128,2560]{1,0:T(8,128)(2,1)S(1)}, bf16[128,2560]{1,0:T(8,128)(2,1)S(1)}, u32[]{:S(2)}, u32[]{:S(2)}) collective-permute-start(bf16[128,2560]{1,0:T(8,128)(2,1)S(1)} %collective-permute-done.34.refs_3_), channel_id=1, source_target_pairs={{0,2},{1,39},{8,10},{9,47},{16,18},{17,55},{24,26},{25,63},{2,4},{... | collective-permute-start | bytes 1966088 | tf_op jit(solution)/shard_map/ppermute | solution.py:33
  96.5 49.2 %copy-start.9 = (bf16[128,2560]{1,0:T(8,128)(2,1)}, bf16[128,2560]{1,0:T(8,128)(2,1)S(1)}, u32[]{:S(2)}) copy-start(bf16[128,2560]{1,0:T(8,128)(2,1)S(1)} %collective-permute-done.35.refs_0_.refs_4_) | copy-start | bytes 1966084
  145.7 0.8 copy-start.10
  146.5 1.1 copy-start.12
  150.7 62.8 %collective-permute-start.41 = (bf16[288,2560]{1,0:T(8,128)(2,1)}, bf16[288,2560]{1,0:T(8,128)(2,1)}, u32[]{:S(2)}, u32[]{:S(2)}) collective-permute-start(bf16[288,2560]{1,0:T(8,128)(2,1)} %choose.7.refs_7_.own), channel_id=1, source_target_pairs={{0,4},{1,5},{8,12},{9,13},{16,20},{17,21},{24,28},{25,29},{2,6},{3... | collective-permute-start | bytes 4423688 | tf_op jit(solution)/shard_map/ppermute | solution.py:33
  157.4 59.2 %collective-permute-start.43 = (bf16[224,2560]{1,0:T(8,128)(2,1)}, bf16[224,2560]{1,0:T(8,128)(2,1)S(1)}, u32[]{:S(2)}, u32[]{:S(2)}) collective-permute-start(bf16[224,2560]{1,0:T(8,128)(2,1)} %get-tuple-element.150), channel_id=1, source_target_pairs={{0,8},{1,9},{8,16},{9,17},{16,24},{17,25},{24,0},{25,1},{2,10},{3,... | collective-permute-start | bytes 3440648 | tf_op jit(solution)/shard_map/ppermute | solution.py:33
  157.5 59.1 %collective-permute-start.44 = (bf16[224,2560]{1,0:T(8,128)(2,1)}, bf16[224,2560]{1,0:T(8,128)(2,1)S(1)}, u32[]{:S(2)}, u32[]{:S(2)}) collective-permute-start(bf16[224,2560]{1,0:T(8,128)(2,1)} %get-tuple-element.151), channel_id=1, source_target_pairs={{0,16},{1,17},{8,24},{9,25},{16,0},{17,1},{24,8},{25,9},{2,18},{3,... | collective-permute-start | bytes 3440648 | tf_op jit(solution)/shard_map/ppermute | solution.py:33
  161.3 55.4 %collective-permute-start.45 = (bf16[224,2560]{1,0:T(8,128)(2,1)}, bf16[224,2560]{1,0:T(8,128)(2,1)}, u32[]{:S(2)}, u32[]{:S(2)}) collective-permute-start(bf16[224,2560]{1,0:T(8,128)(2,1)} %get-tuple-element.142.refs_4_), channel_id=1, source_target_pairs={{0,24},{1,25},{8,0},{9,1},{16,8},{17,9},{24,16},{25,17},{2,26},{3,... | collective-permute-start | bytes 3440648 | tf_op jit(solution)/shard_map/ppermute | solution.py:33
  216.6 1.0 copy-start.2
  216.6 1.4 copy-start.3
  221.9 8.5 %copy-start.1 = (bf16[288,2560]{1,0:T(8,128)(2,1)S(1)}, bf16[288,2560]{1,0:T(8,128)(2,1)}, u32[]{:S(2)}) copy-start(bf16[288,2560]{1,0:T(8,128)(2,1)} %choose.8.own.refs_4_) | copy-start | bytes 4423684
  221.9 8.5 %collective-permute-start.46 = (bf16[448,2560]{1,0:T(8,128)(2,1)}, bf16[448,2560]{1,0:T(8,128)(2,1)}, u32[]{:S(2)}, u32[]{:S(2)}) collective-permute-start(bf16[448,2560]{1,0:T(8,128)(2,1)} %hold.7), channel_id=1, source_target_pairs={{0,1},{1,0},{8,9},{9,8},{16,17},{17,16},{24,25},{25,24},{2,3},{3,2... | collective-permute-start | bytes 6881288 | tf_op jit(solution)/shard_map/ppermute | solution.py:33
  222.3 95.2 %all-to-all-start.1 = ((bf16[8,112,2560]{2,1,0:T(8,128)(2,1)}), bf16[8,112,2560]{2,1,0:T(8,128)(2,1)}, u32[]{:S(2)}, u32[]{:S(2)}) async-start(bf16[8,112,2560]{2,1,0:T(8,128)(2,1)} %down.1.refs_0_.refs_5_), calls=%async_computation.1 | async-start | bytes 9175040 | tf_op jit(solution)/shard_map/all_to_all | solution.py:450
  230.4 34.0 %collective-permute-start.42 = (bf16[288,2560]{1,0:T(8,128)(2,1)S(1)}, bf16[288,2560]{1,0:T(8,128)(2,1)S(1)}, u32[]{:S(2)}, u32[]{:S(2)}) collective-permute-start(bf16[288,2560]{1,0:T(8,128)(2,1)S(1)} %copy-done.1), channel_id=1, source_target_pairs={{0,2},{1,3},{8,10},{9,11},{16,18},{17,19},{24,26},{25,27},{2,0},{3... | collective-permute-start | bytes 4423688 | tf_op jit(solution)/shard_map/ppermute | solution.py:33
  237.1 31.4 %collective-permute-start.47 = (bf16[192,1280]{1,0:T(8,128)(2,1)}, bf16[192,1280]{1,0:T(8,128)(2,1)S(1)}, u32[]{:S(2)}, u32[]{:S(2)}) collective-permute-start(bf16[192,1280]{1,0:T(8,128)(2,1)} %get-tuple-element.153), channel_id=1, source_target_pairs={{0,64},{1,65},{8,72},{9,73},{16,80},{17,81},{24,88},{25,89},{2,66}... | collective-permute-start | bytes 1474568 | tf_op jit(solution)/shard_map/ppermute | solution.py:33
  238.4 30.1 %collective-permute-start.48 = (bf16[192,1280]{1,0:T(8,128)(2,1)}, bf16[192,1280]{1,0:T(8,128)(2,1)S(1)}, u32[]{:S(2)}, u32[]{:S(2)}) collective-permute-start(bf16[192,1280]{1,0:T(8,128)(2,1)} %get-tuple-element.154), channel_id=1, source_target_pairs={{0,128},{1,129},{8,136},{9,137},{16,144},{17,145},{24,152},{25,153... | collective-permute-start | bytes 1474568 | tf_op jit(solution)/shard_map/ppermute | solution.py:33
  241.1 27.4 %collective-permute-start.49 = (bf16[192,1280]{1,0:T(8,128)(2,1)}, bf16[192,1280]{1,0:T(8,128)(2,1)}, u32[]{:S(2)}, u32[]{:S(2)}) collective-permute-start(bf16[192,1280]{1,0:T(8,128)(2,1)} %get-tuple-element.155), channel_id=1, source_target_pairs={{0,192},{1,193},{8,200},{9,201},{16,208},{17,209},{24,216},{25,217... | collective-permute-start | bytes 1474568 | tf_op jit(solution)/shard_map/ppermute | solution.py:33
  264.3 1.1 copy-start.11
  268.5 0.8 copy-start.19
  268.5 0.9 copy-start.20
  272.0 12.5 %collective-permute-start.50 = (bf16[192,1280]{1,0:T(8,128)(2,1)}, bf16[192,1280]{1,0:T(8,128)(2,1)S(1)}, u32[]{:S(2)}, u32[]{:S(2)}) collective-permute-start(bf16[192,1280]{1,0:T(8,128)(2,1)} %sum.2.own), channel_id=1, source_target_pairs={{0,1},{1,0},{8,9},{9,8},{16,17},{17,16},{24,25},{25,24},{2,3},{3,2... | collective-permute-start | bytes 1474568 | tf_op jit(solution)/shard_map/ppermute | solution.py:33
  279.5 38.0 %collective-permute-start.51 = (bf16[192,1280]{1,0:T(8,128)(2,1)}, bf16[192,1280]{1,0:T(8,128)(2,1)S(1)}, u32[]{:S(2)}, u32[]{:S(2)}) collective-permute-start(bf16[192,1280]{1,0:T(8,128)(2,1)} %get-tuple-element.159), channel_id=1, source_target_pairs={{0,64},{1,65},{8,72},{9,73},{16,80},{17,81},{24,88},{25,89},{2,66}... | collective-permute-start | bytes 1474568 | tf_op jit(solution)/shard_map/ppermute | solution.py:33
  280.7 36.7 %collective-permute-start.52 = (bf16[192,1280]{1,0:T(8,128)(2,1)}, bf16[192,1280]{1,0:T(8,128)(2,1)S(1)}, u32[]{:S(2)}, u32[]{:S(2)}) collective-permute-start(bf16[192,1280]{1,0:T(8,128)(2,1)} %get-tuple-element.160), channel_id=1, source_target_pairs={{0,128},{1,129},{8,136},{9,137},{16,144},{17,145},{24,152},{25,153... | collective-permute-start | bytes 1474568 | tf_op jit(solution)/shard_map/ppermute | solution.py:33
  283.4 34.0 %collective-permute-start.53 = (bf16[192,1280]{1,0:T(8,128)(2,1)}, bf16[192,1280]{1,0:T(8,128)(2,1)S(1)}, u32[]{:S(2)}, u32[]{:S(2)}) collective-permute-start(bf16[192,1280]{1,0:T(8,128)(2,1)} %get-tuple-element.161), channel_id=1, source_target_pairs={{0,192},{1,193},{8,200},{9,201},{16,208},{17,209},{24,216},{25,217... | collective-permute-start | bytes 1474568 | tf_op jit(solution)/shard_map/ppermute | solution.py:33
  284.5 0.8 copy-start.21
  301.2 11.8 %collective-permute-start.13 = (bf16[96,1280]{1,0:T(8,128)(2,1)S(1)}, bf16[96,1280]{1,0:T(8,128)(2,1)S(1)}, u32[]{:S(2)}, u32[]{:S(2)}) collective-permute-start(bf16[96,1280]{1,0:T(8,128)(2,1)S(1)} %get-tuple-element.94), channel_id=1, source_target_pairs={{0,14},{1,15},{8,6},{9,7},{16,30},{17,31},{24,22},{25,23},{2,12},{... | collective-permute-start | bytes 737288 | tf_op jit(solution)/shard_map/cond/branch_7_fun/ppermute | solution.py:33
  303.9 11.7 %collective-permute-start.14 = (bf16[96,1280]{1,0:T(8,128)(2,1)S(1)}, bf16[96,1280]{1,0:T(8,128)(2,1)}, u32[]{:S(2)}, u32[]{:S(2)}) collective-permute-start(bf16[96,1280]{1,0:T(8,128)(2,1)S(1)} %get-tuple-element.95), channel_id=1, source_target_pairs={{0,46},{1,47},{8,38},{9,39},{16,62},{17,63},{24,54},{25,55},{2,44}... | collective-permute-start | bytes 737288 | tf_op jit(solution)/shard_map/cond/branch_7_fun/ppermute | solution.py:33
  317.4 0.8 copy-start.16
  317.4 0.9 copy-start.17
  317.4 1.1 copy-start.18
  321.0 16.3 %collective-permute-start.54 = (bf16[192,1280]{1,0:T(8,128)(2,1)}, bf16[192,1280]{1,0:T(8,128)(2,1)S(1)}, u32[]{:S(2)}, u32[]{:S(2)}) collective-permute-start(bf16[192,1280]{1,0:T(8,128)(2,1)} %sum.3.own), channel_id=1, source_target_pairs={{0,1},{1,0},{8,9},{9,8},{16,17},{17,16},{24,25},{25,24},{2,3},{3,2... | collective-permute-start | bytes 1474568 | tf_op jit(solution)/shard_map/ppermute | solution.py:33
  334.6 28.7 %collective-permute-start.38 = (bf16[128,2560]{1,0:T(8,128)(2,1)}, bf16[128,2560]{1,0:T(8,128)(2,1)S(1)}, u32[]{:S(2)}, u32[]{:S(2)}) collective-permute-start(bf16[128,2560]{1,0:T(8,128)(2,1)} %get-tuple-element.145), channel_id=1, source_target_pairs={{0,38},{1,3},{8,46},{9,11},{16,54},{17,19},{24,62},{25,27},{2,0},{... | collective-permute-start | bytes 1966088 | tf_op jit(solution)/shard_map/ppermute | solution.py:33
  335.2 33.6 %collective-permute-start.40 = (bf16[128,2560]{1,0:T(8,128)(2,1)}, bf16[128,2560]{1,0:T(8,128)(2,1)S(1)}, u32[]{:S(2)}, u32[]{:S(2)}) collective-permute-start(bf16[128,2560]{1,0:T(8,128)(2,1)} %get-tuple-element.147), channel_id=1, source_target_pairs={{0,2},{1,39},{8,10},{9,47},{16,18},{17,55},{24,26},{25,63},{2,4},{... | collective-permute-start | bytes 1966088 | tf_op jit(solution)/shard_map/ppermute | solution.py:33
  337.3 0.8 copy-start.22
  341.2 22.2 %copy-start.15 = (bf16[128,2560]{1,0:T(8,128)(2,1)S(1)}, bf16[128,2560]{1,0:T(8,128)(2,1)}, u32[]{:S(2)}) copy-start(bf16[128,2560]{1,0:T(8,128)(2,1)} %get-tuple-element.146) | copy-start | bytes 1966084
  341.3 18.4 %collective-permute-start.28 = (bf16[96,1280]{1,0:T(8,128)(2,1)S(1)}, bf16[96,1280]{1,0:T(8,128)(2,1)S(1)}, u32[]{:S(2)}, u32[]{:S(2)}) collective-permute-start(bf16[96,1280]{1,0:T(8,128)(2,1)S(1)} %get-tuple-element.110), channel_id=1, source_target_pairs={{0,14},{1,15},{8,6},{9,7},{16,30},{17,31},{24,22},{25,23},{2,12},{... | collective-permute-start | bytes 737288 | tf_op jit(solution)/shard_map/cond/branch_7_fun/ppermute | solution.py:33
  342.0 20.2 %collective-permute-start.29 = (bf16[96,1280]{1,0:T(8,128)(2,1)S(1)}, bf16[96,1280]{1,0:T(8,128)(2,1)}, u32[]{:S(2)}, u32[]{:S(2)}) collective-permute-start(bf16[96,1280]{1,0:T(8,128)(2,1)S(1)} %get-tuple-element.111), channel_id=1, source_target_pairs={{0,46},{1,47},{8,38},{9,39},{16,62},{17,63},{24,54},{25,55},{2,44}... | collective-permute-start | bytes 737288 | tf_op jit(solution)/shard_map/cond/branch_7_fun/ppermute | solution.py:33
  362.2 4.9 %copy-start = (bf16[288,2560]{1,0:T(8,128)(2,1)S(1)}, bf16[288,2560]{1,0:T(8,128)(2,1)}, u32[]{:S(2)}) copy-start(bf16[288,2560]{1,0:T(8,128)(2,1)} %choose.9.refs_0_) | copy-start | bytes 4423684
  362.2 4.9 %copy-start.5 = (f32[96,1280]{1,0:T(8,128)S(1)}, f32[96,1280]{1,0:T(8,128)}, u32[]{:S(2)}) copy-start(f32[96,1280]{1,0:T(8,128)} %convert_add_fusion.1.refs_1_) | copy-start | bytes 1474564
  363.6 11.4 %copy-start.13 = (f32[128,2560]{1,0:T(8,128)S(1)}, f32[128,2560]{1,0:T(8,128)}, u32[]{:S(2)}) copy-start(f32[128,2560]{1,0:T(8,128)} %get-tuple-element.144) | copy-start | bytes 3932164
  363.6 11.4 %collective-permute-start.39 = (bf16[128,2560]{1,0:T(8,128)(2,1)S(1)}, bf16[128,2560]{1,0:T(8,128)(2,1)S(1)}, u32[]{:S(2)}, u32[]{:S(2)}) collective-permute-start(bf16[128,2560]{1,0:T(8,128)(2,1)S(1)} %add_convert_fusion.1), channel_id=1, source_target_pairs={{0,38},{1,3},{8,46},{9,11},{16,54},{17,19},{24,62},{25,27},{2,0},{... | collective-permute-start | bytes 1966088 | tf_op jit(solution)/shard_map/ppermute | solution.py:33
Sparse Core Ops, SparseCore 0:
  50.7 110.4 all-gather.1
